TPU v7x, 32 devices: a whole 2x2x4 slice. The times are simulated.
32 devices in a mesh: parts: 2 (over y), ctx: 4 (over z), grid: 4 (over x, core).
Axes of the slice: x: 2, y: 2, z: 4, core: 2. Of those that a mesh axis runs over, the one named last changes fastest.
Arguments:
- frames_in: bfloat16 [4096, 1536], P(('parts', 'ctx'), 'grid'), parts along dimension 0, may hold values from -230 to 230
- norm1_gain: bfloat16 [1536], P('grid'), may hold values from 0.25 to 1.75
- norm1_bias: bfloat16 [1536], P('grid'), may hold values from -3 to 3
- w_query: bfloat16 [1536, 1536], P(None, 'grid'), may hold values from -0.5 to 0.5
- w_key: bfloat16 [1536, 1536], P(None, 'grid'), may hold values from -2 to 2
- w_value: bfloat16 [1536, 1536], P(None, 'grid'), may hold values from -0.15625 to 0.15625
- w_out: bfloat16 [1536, 1536], P('grid'), may hold values from -0.15625 to 0.15625
- norm2_gain: bfloat16 [1536], P('grid'), may hold values from 0.099609375 to 1.8984375
- norm2_bias: bfloat16 [1536], P('grid'), may hold values from -3 to 3
- w_glu_value: bfloat16 [1536, 1536], P(None, 'grid'), may hold values from -0.15625 to 0.15625
- w_glu_gate: bfloat16 [1536, 1536], P(None, 'grid'), may hold values from -0.15625 to 0.15625
- depth_kernel: float32 [31, 1536], P(None, 'grid'), may hold values from -1 to 1
- bn_scale: float32 [1536], P('grid'), may hold values from 0.25 to 1.75
- bn_shift: float32 [1536], P('grid'), may hold values from -3 to 3
- w_proj: bfloat16 [1536, 1536], P('grid'), may hold values from -0.3125 to 0.3125
Outputs:
- layer_out: bfloat16 [4096, 1536], P(('parts', 'ctx'), 'grid'), parts along dimension 0
There are 2 independent parts, one for each index of `parts`. A program takes and returns all parts, laid end to end along the dimension named above; an argument that names none is the same for every part. Nothing has to cross between parts.
All inputs are finite; a program needn't handle non-finite values.
Results may differ from a plain program's by a relative error of at most 0.009.
Values may be sent and summed in bfloat16 or wider, within the bound.
No kernel may reach another device: no remote copies, remote signals or barrier semaphores. Data moves between devices by JAX's collectives and lax.ppermute only.
A program may use at most 256 MiB of HBM per device.

v0:
```python
import functools
import math

import jax
import jax.numpy as jnp
from jax import lax
from jax.experimental import pallas as pl
from jax.experimental.pallas import tpu as pltpu
from jax.sharding import PartitionSpec as P

HEAD_DIM = 64
PAIR = 2 * HEAD_DIM
KERNEL = 31
HALF = 15
HALO = 16
EPSILON = 1e-05
CORES = 2
VMEM_BYTES = 16 * 1024 * 1024
BF16 = jnp.bfloat16
F32 = jnp.float32
SCORE_SCALE = math.log2(math.e) / math.sqrt(HEAD_DIM)


def exchange(cells, axis, distance):
    count = lax.axis_size(axis)
    return lax.ppermute(cells, axis, [(i, i ^ distance) for i in range(count)])


def kernel_call(body, outs, operands, spaces=None, scratch=(), aliases=None):
    spaces = spaces or {}
    operands = [
        pltpu.with_memory_space_constraint(cells, pltpu.HBM) if spaces.get(i) == pltpu.HBM else cells
        for i, cells in enumerate(operands)
    ]
    in_specs = [
        pl.BlockSpec(memory_space=spaces.get(i, pltpu.VMEM)) for i in range(len(operands))
    ]
    return pl.pallas_call(
        body,
        in_specs=in_specs,
        out_specs=tuple(pl.BlockSpec(memory_space=pltpu.VMEM) for _ in outs),
        out_shape=tuple(jax.ShapeDtypeStruct(shape, dtype) for shape, dtype in outs),
        scratch_shapes=list(scratch),
        input_output_aliases=aliases or {},
        compiler_params=pltpu.CompilerParams(vmem_limit_bytes=VMEM_BYTES),
        cost_estimate=pl.CostEstimate(flops=1000, bytes_accessed=1000, transcendentals=0),
    )(*operands)


def after(cells, *done):
    def body(*refs):
        pass

    anywhere = pl.BlockSpec(memory_space=pl.ANY)
    return pl.pallas_call(
        body,
        in_specs=[anywhere] * (1 + len(done)),
        out_specs=anywhere,
        out_shape=jax.ShapeDtypeStruct(cells.shape, cells.dtype),
        input_output_aliases={0: 0},
        compiler_params=pltpu.CompilerParams(vmem_limit_bytes=64 * 1024),
        cost_estimate=pl.CostEstimate(flops=0, bytes_accessed=0, transcendentals=0),
    )(cells, *done)


def fold_kernel(order, which, count, me_ref, gains_ref, *refs):
    sources, (folded_ref, sums_ref), weights, done = refs[:count], refs[count : count + 2], refs[count + 2 : -1], refs[-1]
    copies = [pltpu.make_async_copy(sources[n], weights[n], done.at[n]) for n in range(count)]
    for copy in copies:
        copy.start()
    width = gains_ref.shape[1]
    columns = weights[0].shape[1]
    factors = []
    for r in order:
        gains = gains_ref[pl.ds(pl.multiple_of((me_ref[0] ^ r) * 8, 8), 8), :]
        gain = jnp.transpose(jnp.broadcast_to(gains[which : which + 1, :], (PAIR, width)))
        bias = jnp.broadcast_to(gains[which + 1 : which + 2, :], (8, width)).astype(BF16)
        factors.append((gain, bias))
    for n, ref in enumerate(weights):
        copies[n].wait()
        total = jnp.zeros((8, columns), F32)
        for k, r in enumerate(order):
            gain, bias = factors[k]
            start = pl.multiple_of((me_ref[0] ^ r) * width, width)
            block = ref[pl.ds(start, width), :]
            total = total + jnp.dot(bias, block, preferred_element_type=F32)
            for j in range(columns // PAIR):
                target = (j * count + n) * PAIR
                folded_ref[k * width : (k + 1) * width, target : target + PAIR] = (
                    block[:, j * PAIR : (j + 1) * PAIR].astype(F32) * gain
                ).astype(BF16)
        for j in range(columns // PAIR):
            target = (j * count + n) * PAIR
            sums_ref[1:2, target : target + PAIR] = total[0:1, j * PAIR : (j + 1) * PAIR]
    sums = jnp.dot(jnp.ones((8, folded_ref.shape[0]), BF16), folded_ref[...], preferred_element_type=F32)
    sums_ref[0:1, :] = sums[0:1]


def folded(me, order, which, gains, weights):
    rows, columns = weights[0].shape
    total = columns * len(weights)
    spaces = {2 + n: pltpu.HBM for n in range(len(weights))}
    return kernel_call(
        functools.partial(fold_kernel, order, which, len(weights)),
        [((rows, total), BF16), ((2, total), F32)],
        [me, gains, *weights],
        spaces={0: pltpu.SMEM, **spaces},
        scratch=[pltpu.VMEM((rows, columns), BF16)] * len(weights) + [pltpu.SemaphoreType.DMA((len(weights),))],
    )


def stack_kernel(*refs):
    count = (len(refs) - 2) // 2
    sources, out_ref, rows, done = refs[:count], refs[count], refs[count + 1 : -1], refs[-1]
    copies = [pltpu.make_async_copy(sources[i], rows[i], done.at[i]) for i in range(count)]
    for copy in copies:
        copy.start()
    out_ref[...] = jnp.zeros_like(out_ref)
    for i, copy in enumerate(copies):
        copy.wait()
        out_ref[i : i + 1, :] = rows[i][...].astype(F32).reshape(1, out_ref.shape[1])


def reorder_kernel(order, me_ref, source_ref, out_ref, done):
    width = source_ref.shape[1] // len(order)
    copies = []
    for k, r in enumerate(order):
        cols = pl.ds(pl.multiple_of((me_ref[0] ^ r) * width, PAIR), width)
        copies.append(
            pltpu.make_async_copy(source_ref.at[:, cols], out_ref.at[:, k * width : (k + 1) * width], done.at[k])
        )
        copies[-1].start()
    for copy in copies:
        copy.wait()


def half_kernel(part_ref, source_ref, half_ref, done):
    rows = half_ref.shape[0]
    copy = pltpu.make_async_copy(
        source_ref.at[pl.ds(pl.multiple_of(part_ref[0] * rows, rows), rows), :], half_ref, done.at[0]
    )
    copy.start()
    copy.wait()


def row_statistics(refs):
    rows, width = refs[0].shape
    full = width * len(refs)
    means, scales = [], []
    step = math.gcd(rows, 64)
    for start in range(0, rows, step):
        parts = [ref[start : start + step, :].astype(F32) for ref in refs]
        mean = sum(jnp.sum(part, axis=1, keepdims=True) for part in parts) / full
        variance = sum(jnp.sum(jnp.square(part - mean), axis=1, keepdims=True) for part in parts) / full
        means.append(mean)
        scales.append(lax.rsqrt(variance + EPSILON))
    return jnp.concatenate(means, axis=0), jnp.concatenate(scales, axis=0)


def norm_product(cells, mean, scale, folded_ref, sums_ref, start, columns):
    cols = slice(start, start + columns)
    product = jnp.dot(cells, folded_ref[:, cols], preferred_element_type=F32)
    return (product - mean * sums_ref[0:1, cols]) * scale + sums_ref[1:2, cols]


def lane_masks():
    lanes = lax.broadcasted_iota(jnp.int32, (1, PAIR), 1)
    return lanes < HEAD_DIM


def keys_values(projected):
    low = lane_masks()
    values = projected[:, PAIR : 2 * PAIR]
    return (
        projected[:, :PAIR].astype(BF16),
        jnp.where(low, values, 1.0).astype(BF16),
        jnp.where(low, 1.0, values).astype(BF16),
    )


def project_kernel(count, first, *refs):
    blocks, (folded_ref, sums_ref, *refs) = refs[:count], refs[count:]
    key_ref, value_ref = refs[-2:]
    query_ref = refs[-3] if first else None
    mean, scale = row_statistics(blocks)
    cells = jnp.concatenate([ref[...] for ref in blocks], axis=1)
    low = lane_masks()
    for j in range(key_ref.shape[1] // PAIR):
        columns = (3 if first else 2) * PAIR
        projected = norm_product(cells, mean, scale, folded_ref, sums_ref, j * 3 * PAIR, columns)
        base = 2 * j * PAIR
        (
            key_ref[:, j * PAIR : (j + 1) * PAIR],
            value_ref[:, base : base + PAIR],
            value_ref[:, base + PAIR : base + 2 * PAIR],
        ) = keys_values(projected)
        if first:
            queries = projected[:, 2 * PAIR :] * SCORE_SCALE
            query_ref[:, base : base + PAIR] = jnp.where(low, queries, 0.0).astype(BF16)
            query_ref[:, base + PAIR : base + 2 * PAIR] = jnp.where(low, 0.0, queries).astype(BF16)


def rows_of(ref, spans, cols):
    return jnp.concatenate([ref[start : start + size, cols] for start, size in spans], axis=0)


def attend_pair(pair, spans, query_ref, keys, values, state_ref):
    for head in range(2):
        index = 2 * pair + head
        queries = rows_of(query_ref, spans, slice(index * PAIR, (index + 1) * PAIR))
        scores = lax.dot_general(queries, keys, (((1,), (1,)), ((), ())), preferred_element_type=F32)
        peak = jnp.max(scores, axis=1, keepdims=True)
        soft = jnp.exp2(scores - peak).astype(BF16)
        sums = jnp.dot(soft, values[head], preferred_element_type=F32)
        state_ref[:, 2 * index * PAIR : (2 * index + 1) * PAIR] = sums
        state_ref[:, (2 * index + 1) * PAIR : (2 * index + 2) * PAIR] = jnp.broadcast_to(peak, (peak.shape[0], PAIR))


def merge_head(old_ref, part_ref, spans, index):
    sums = slice(2 * index * PAIR, (2 * index + 1) * PAIR)
    peaks = slice((2 * index + 1) * PAIR, (2 * index + 2) * PAIR)
    old_peak, part_peak = rows_of(old_ref, spans, peaks), part_ref[:, peaks]
    peak = jnp.maximum(old_peak, part_peak)
    total = rows_of(old_ref, spans, sums) * jnp.exp2(old_peak - peak) + part_ref[:, sums] * jnp.exp2(part_peak - peak)
    return total, peak


def attend_kernel(first, last, spans, query_ref, key_ref, value_ref, *refs):
    if last:
        old_ref, attended, part = refs[0], refs[-2], refs[-1]
    elif first:
        part, token_ref = refs[-2:]
    else:
        old_ref, (state_ref, token_ref, part) = refs[0], refs[-3:]
    if not last:
        token_ref[...] = jnp.zeros_like(token_ref)
    pairs = query_ref.shape[1] // (2 * PAIR)
    for j in range(pairs):
        values = [value_ref[:, n * PAIR : (n + 1) * PAIR] for n in (2 * j, 2 * j + 1)]
        attend_pair(j, spans, query_ref, key_ref[:, j * PAIR : (j + 1) * PAIR], values, part)
    if first:
        return
    low = lane_masks()
    for j in range(pairs):
        heads = [merge_head(old_ref, part, spans, 2 * j + head) for head in range(2)]
        if last:
            (one, _), (two, _) = heads
            both = jnp.where(low, one, two)
            weight = pltpu.roll(jnp.where(low, two, one), HEAD_DIM, 1)
            attended[:, j * PAIR : (j + 1) * PAIR] = (both / weight).astype(BF16)
        else:
            for head, (sums, peak) in enumerate(heads):
                at = 2 * (2 * j + head) * PAIR
                state_ref[:, at : at + PAIR] = sums
                state_ref[:, at + PAIR : at + 2 * PAIR] = peak


def middle_kernel(count, order, spans, me_ref, part_ref, odd_ref, *refs):
    attended, frames_refs, refs = refs[:count], refs[count : 2 * count], refs[2 * count :]
    *pieces, folded_ref, sums_ref, own_ref, out_ref, near_ref, far_ref, middle = refs
    total = out_ref.shape[0]
    width = frames_refs[0].shape[1]
    cells = jnp.concatenate([ref[:, :width] for ref in attended], axis=1)
    swap = part_ref[0] != 0

    def weights(k):
        if width % PAIR:
            cols = slice(k * width, (k + 1) * width)
        else:
            cols = pl.ds(pl.multiple_of((me_ref[0] ^ order[k]) * width, PAIR), width)
        rows, index = [], 0
        while index < len(pieces):
            mine = pieces[index][:, cols]
            index += 1
            if mine.shape[0] < width:
                other = pieces[index][:, cols]
                index += 1
                mine = jnp.concatenate([jnp.where(swap, other, mine), jnp.where(swap, mine, other)], axis=0)
            rows.append(mine)
        return jnp.concatenate(rows, axis=0)

    for k in range(0, count, 2):
        both = jnp.concatenate([weights(k), weights(k + 1)], axis=1)
        share = jnp.dot(cells, both, preferred_element_type=F32)
        for n in range(2):
            cols = slice((k + n) * width, (k + n + 1) * width)
            own = jnp.concatenate([frames_refs[k + n][start : start + size, :] for start, size in spans], axis=0)
            middle[:, cols] = (own.astype(F32) + share[:, n * width : (n + 1) * width]).astype(BF16)
    own_ref[...] = middle[:, :width]
    mean, scale = row_statistics((middle,))
    cells = middle[...]
    for j in range(out_ref.shape[1] // PAIR):
        both = norm_product(cells, mean, scale, folded_ref, sums_ref, j * 2 * PAIR, 2 * PAIR)
        out_ref[:, j * PAIR : (j + 1) * PAIR] = (
            both[:, :PAIR] / (1.0 + jnp.exp(-both[:, PAIR:]))
        ).astype(BF16)
    odd = odd_ref[0] != 0
    head, tail = out_ref[:HALO, :], out_ref[total - HALO :, :]
    near_ref[...] = jnp.where(odd, head, tail)
    far_ref[...] = jnp.where(odd, tail, head)


def conv_rows(padded, start, piece, cols, taps, scale, shift):
    window = padded[pl.ds(start, piece + 2 * HALO), cols]
    convolved = None
    for residue in range(8):
        part = None
        for offset in range(residue, KERNEL + 1, 8):
            if offset == 0:
                continue
            base = offset - residue
            term = taps[offset - 1] * window[base : base + piece + 8]
            part = term if part is None else part + term
        part = part[residue : residue + piece]
        convolved = part if convolved is None else convolved + part
    value = convolved * scale + shift
    return (value / (1.0 + jnp.exp(-value))).astype(BF16)


def conv_kernel(outer, first_ref, second_ref, *refs):
    if outer:
        odd_ref, near_ref, far_ref, *refs = refs
        odd, near, far = odd_ref[0] != 0, near_ref[...], far_ref[...]
    taps_ref, bn_ref, w_ref, keep_ref, send_ref, padded, activated = refs
    total, width = first_ref.shape
    half = keep_ref.shape[1]
    piece, quarter = 32, total // 2
    if outer:
        runs = (
            (jnp.where(odd, near, far), first_ref[:quarter, :], second_ref[:HALO, :]),
            (second_ref[total - HALO :, :], first_ref[quarter:, :], jnp.where(odd, far, near)),
        )
    else:
        runs = ((first_ref[quarter - HALO : quarter, :], second_ref[...], first_ref[quarter : quarter + HALO, :]),)
    at = 0
    for before, rows, behind in runs:
        count = rows.shape[0]
        padded[0:HALO, :] = before.astype(F32)
        padded[HALO : HALO + count, :] = rows.astype(F32)
        padded[HALO + count : 2 * HALO + count, :] = behind.astype(F32)
        for col in range(0, width, PAIR):
            cols = slice(col, col + PAIR)
            taps = [taps_ref[j : j + 1, cols] for j in range(KERNEL)]
            scale, shift = bn_ref[0:1, cols], bn_ref[1:2, cols]

            def block(index, carry, at=at):
                start = pl.multiple_of(index * piece, piece)
                target = pl.multiple_of(at + index * piece, piece)
                activated[pl.ds(target, piece), cols] = conv_rows(padded, start, piece, cols, taps, scale, shift)
                return carry

            lax.fori_loop(0, count // piece, block, 0, unroll=4)
        at += count
    share = activated[...]
    send_ref[...] = jnp.dot(share, w_ref[:, half:], preferred_element_type=F32).astype(BF16)
    keep_ref[...] = jnp.dot(share, w_ref[:, :half], preferred_element_type=F32).astype(BF16)


def pad_columns(weight, width):
    if weight.shape[1] == width:
        return weight
    return jnp.pad(weight, ((0, 0), (0, width - weight.shape[1])))


def on_device(
    frames_in,
    norm1_gain,
    norm1_bias,
    w_query,
    w_key,
    w_value,
    w_out,
    norm2_gain,
    norm2_bias,
    w_glu_value,
    w_glu_gate,
    depth_kernel,
    bn_scale,
    bn_shift,
    w_proj,
):
    frames, width = frames_in.shape
    grid, ctx = lax.axis_size("grid"), lax.axis_size("ctx")
    me = lax.axis_index("grid")
    place = me.astype(jnp.int32).reshape(1)
    odd = (lax.axis_index("ctx") % 2).astype(jnp.int32).reshape(1)
    order = list(range(0, grid, CORES)) + list(range(1, grid, CORES))
    padded = -(-width // PAIR) * PAIR
    every = ((0, frames),)

    def by_distance(cells):
        return jnp.concatenate(
            [lax.dynamic_slice_in_dim(cells, (me ^ r) * width, width, 1) for r in order], axis=1
        )

    def over_chips(block):
        return [exchange(block, "grid", CORES * a) for a in range(1, grid // CORES)]

    def other_core(blocks):
        return [exchange(block, "grid", 1) for block in blocks]

    vectors = [norm1_gain, norm1_bias, norm2_gain, norm2_bias]
    (gains,) = kernel_call(
        stack_kernel,
        [((8, width), F32)],
        vectors,
        spaces={i: pltpu.HBM for i in range(len(vectors))},
        scratch=[pltpu.VMEM((width,), BF16)] * len(vectors) + [pltpu.SemaphoreType.DMA((len(vectors),))],
    )
    gains = lax.all_gather(gains, "grid", axis=0, tiled=True)
    raw = {0: frames_in}
    chips = {0: over_chips(frames_in)}
    for k in reversed(range(ctx.bit_length() - 1)):
        raw[1 << k] = exchange(frames_in, "ctx", 1 << k)

    w_query, w_key, w_value, w_glu_value, w_glu_gate = (
        pad_columns(weight, padded) for weight in (w_query, w_key, w_value, w_glu_value, w_glu_gate)
    )
    if width % PAIR:
        row_pad = ((0, padded - width), (0, 0))
        w_p = jnp.pad(by_distance(w_proj), row_pad)
    else:
        (w_p,) = kernel_call(
            functools.partial(reorder_kernel, order),
            [(w_proj.shape, BF16)],
            [place, w_proj],
            spaces={0: pltpu.SMEM, 1: pltpu.HBM},
            scratch=[pltpu.SemaphoreType.DMA((grid,))],
        )
    taps = pad_columns(depth_kernel, padded)
    bn = pad_columns(jnp.stack([bn_scale, bn_shift]), padded)
    qkv, qkv_sums = folded(place, order, 0, gains, (w_key, w_value, w_query))
    chips[0] = [after(block, qkv_sums) for block in chips[0]]
    glu, glu_sums = folded(place, order, 2, gains, (w_glu_value, w_glu_gate))

    parts = lax.axis_size("parts")
    part = lax.axis_index("parts").astype(jnp.int32).reshape(1)
    if parts == 2:
        (half,) = kernel_call(
            half_kernel,
            [((width // 2, w_out.shape[1]), BF16)],
            [part, w_out],
            spaces={0: pltpu.SMEM, 1: pltpu.HBM},
            scratch=[pltpu.SemaphoreType.DMA((1,))],
        )
    else:
        half = w_out
    crossed = over_chips(after(half, *chips[0]))
    state_shape = ((frames, 4 * padded), F32)
    token_shape = ((8, 128), F32)
    wide, narrow = ((frames, 2 * padded), BF16), ((frames, padded), BF16)
    chips[1] = [exchange(block, "ctx", 1) for block in chips[0]]
    own = [frames_in] + chips[0]
    own_blocks = own + other_core(own)
    n = len(own_blocks)
    early = [*[raw[s] for s in raw if s], glu_sums, w_p]
    queries, keys, values = kernel_call(
        functools.partial(project_kernel, n, True),
        [wide, narrow, wide],
        [*own_blocks, qkv, qkv_sums, *early],
        spaces={n + 2 + i: pl.ANY for i in range(len(early))},
    )
    def prepare(s, done):
        if 2 <= s < ctx:
            low = s & -s
            if s != low:
                raw[s] = after(exchange(raw[s ^ low], "ctx", low), done)
            chips[s] = over_chips(raw[s])

    prepare(2, None)
    state, token = kernel_call(
        functools.partial(attend_kernel, True, False, every),
        [state_shape, token_shape],
        [queries, keys, values, *crossed],
        spaces={3 + i: pl.ANY for i in range(len(crossed))},
    )
    crossed = [after(block, token) for block in crossed]
    swapped = [exchange(block, "parts", 1) for block in crossed] if parts == 2 else []
    moved = {1: [after(block, token) for block in chips[1]]}
    for s in range(1, ctx):
        last = s == ctx - 1
        mine = [raw[s]] + moved[s]
        keys, values = kernel_call(
            functools.partial(project_kernel, n, False),
            [narrow, wide],
            [*mine, *other_core(mine), qkv, qkv_sums],
        )
        if last:
            break
        prepare(s + 2, token)
        moved[s + 1] = [after(block, token) for block in chips[s + 1]]
        behind = [raw[s + 2]] if s + 2 < ctx else []
        behind += moved[s + 1]
        state, token = kernel_call(
            functools.partial(attend_kernel, False, False, every),
            [state_shape, token_shape],
            [queries, keys, values, state, *behind],
            spaces={4 + i: pl.ANY for i in range(len(behind))},
            aliases={3: 0},
            scratch=[pltpu.VMEM(*state_shape)],
        )
    rows, quarter = frames // 2, frames // 4
    spans = (((0, quarter), (3 * quarter, quarter)), ((quarter, rows),))
    attended = []
    for h in range(2):
        (mine,) = kernel_call(
            functools.partial(attend_kernel, False, True, spans[h]),
            [((rows, padded), BF16)],
            [queries, keys, values, state],
            scratch=[pltpu.VMEM((rows, 4 * padded), F32)],
        )
        attended.append([mine] + over_chips(mine))
    swapped = [after(block, attended[0][0]) for block in swapped]
    pieces = [w_out]
    for a, block in enumerate(crossed):
        pieces += [block, swapped[a]] if swapped else [block]
    pieces = pieces + other_core(pieces)
    if width % PAIR:
        pieces = [by_distance(piece) for piece in pieces]
    middle, gated = [], []
    for h in range(2):
        mine = attended[h]
        done = gated[0] if h else attended[1][0]
        mine = mine[:1] + [after(block, done) for block in mine[1:]]
        results = kernel_call(
            functools.partial(middle_kernel, n, order, spans[h]),
            [((rows, width), BF16), ((rows, padded), BF16), ((HALO, padded), BF16), ((HALO, padded), BF16)],
            [place, part, odd, *mine, *other_core(mine), *own_blocks, *pieces, glu, glu_sums],
            spaces={0: pltpu.SMEM, 1: pltpu.SMEM, 2: pltpu.SMEM},
            scratch=[pltpu.VMEM((rows, grid * width), BF16)],
        )
        middle.append(results[0])
        gated.append(results[1])
        if h == 0:
            near = exchange(results[2], "ctx", 1)
            between = [(i, i + 1) for i in range(1, ctx - 1, 2)]
            far = lax.ppermute(results[3], "ctx", between + [(b, a) for a, b in between])
    outs = [None, None]
    for h, around in ((1, []), (0, [odd, near, far])):
        keep, send = kernel_call(
            functools.partial(conv_kernel, h == 0),
            [((rows, grid // CORES * width), BF16)] * 2,
            [*gated, *around, taps, bn, w_p],
            spaces={} if h else {2: pltpu.SMEM},
            scratch=[pltpu.VMEM((rows + 2 * HALO, padded), F32), pltpu.VMEM((rows, padded), BF16)],
        )
        theirs = exchange(send, "grid", 1)

        def pair_sum(a):
            cols = slice(a * width, (a + 1) * width)
            return keep[:, cols].astype(F32) + theirs[:, cols].astype(F32)

        result = middle[h].astype(F32) + pair_sum(0)
        for a in range(1, grid // CORES):
            result = result + exchange(pair_sum(a).astype(BF16), "grid", CORES * a).astype(F32)
        outs[h] = result.astype(BF16)
    return jnp.concatenate([outs[0][:quarter], outs[1], outs[0][quarter:]], axis=0)


def solution(mesh):
    return jax.shard_map(
        on_device,
        mesh=mesh,
        in_specs=(
            P(("parts", "ctx"), "grid"),
            P("grid"),
            P("grid"),
            P(None, "grid"),
            P(None, "grid"),
            P(None, "grid"),
            P("grid", None),
            P("grid"),
            P("grid"),
            P(None, "grid"),
            P(None, "grid"),
            P(None, "grid"),
            P("grid"),
            P("grid"),
            P("grid", None),
        ),
        out_specs=P(("parts", "ctx"), "grid"),
        check_vma=False,
    )
```

profile of v0, /device:TPU:0, one launch (start us, length us, event | category | flops | bytes accessed | tf_op | source)
XLA Modules:
  0.0 107.1 jit_solution(13989238570645418013)
XLA Ops:
  0.0 2.9 %collective-permute-start = (bf16[512,384]{1,0:T(8,128)(2,1)}, bf16[512,384]{1,0:T(8,128)(2,1)S(1)}, u32[]{:S(2)}, u32[]{:S(2)}) collective-permute-start(bf16[512,384]{1,0:T(8,128)(2,1)} %refs_4_.3), channel_id=1, source_target_pairs={{0,2},{1,3},{2,0},{3,1},{4,6},{5,7},{6,4},{7,5},{8,10},{9,11},{10,... | collective-permute-start | bytes 1179656 | tf_op jit(solution)/shard_map/ppermute | solution.py:26
  2.9 2.6 %collective-permute-start.3 = (bf16[512,384]{1,0:T(8,128)(2,1)}, bf16[512,384]{1,0:T(8,128)(2,1)}, u32[]{:S(2)}, u32[]{:S(2)}) collective-permute-start(bf16[512,384]{1,0:T(8,128)(2,1)} %refs_4_.3), channel_id=1, source_target_pairs={{0,8},{4,12},{8,0},{12,4},{1,9},{5,13},{9,1},{13,5},{2,10},{6,14},... | collective-permute-start | bytes 1179656 | tf_op jit(solution)/shard_map/ppermute | solution.py:26
  5.5 1.6 %collective-permute-start.4 = (bf16[512,384]{1,0:T(8,128)(2,1)}, bf16[512,384]{1,0:T(8,128)(2,1)}, u32[]{:S(2)}, u32[]{:S(2)}) collective-permute-start(bf16[512,384]{1,0:T(8,128)(2,1)} %refs_4_.3), channel_id=1, source_target_pairs={{0,4},{4,0},{8,12},{12,8},{1,5},{5,1},{9,13},{13,9},{2,6},{6,2},{1... | collective-permute-start | bytes 1179656 | tf_op jit(solution)/shard_map/ppermute | solution.py:26
  7.1 1.9 %shard_map.151.refs_0_ = bf16[192,1536]{1,0:T(8,128)(2,1)} custom-call(s32[1]{0:T(128)} %bitcast.1.part_ref, bf16[384,1536]{1,0:T(8,128)(2,1)} %refs_8_.3), custom_call_target="tpu_custom_call" | custom-call | flops 1000 | bytes 1000 | tf_op jit(solution)/shard_map/pallas_call | solution.py:38
  9.0 0.8 shard_map.145
  9.8 5.2 %all_gather.3.gains_ref = f32[32,384]{1,0:T(8,128)S(1)} all-gather(f32[8,384]{1,0:T(8,128)S(1)} %shard_map.145), channel_id=1, replica_groups=mesh['parts'=2,'ctx'=4,'grid'=4] {'grid'}, dimensions={0}, use_global_device_ids=true | all-gather | bytes 61440 | tf_op jit(solution)/shard_map/all_gather | solution.py:410
  15.0 3.0 %shard_map.146 = (bf16[1536,1152]{1,0:T(8,128)(2,1)S(1)}, f32[2,1152]{1,0:T(2,128)S(1)}) custom-call(s32[1]{0:T(128)} %bitcast.me_ref, f32[32,384]{1,0:T(8,128)S(1)} %all_gather.3.gains_ref, bf16[1536,384]{1,0:T(8,128)(2,1)} %refs_0_.6, bf16[1536,384]{1,0:T(8,128)(2,1)} %refs_1_.4, bf16[1536,384]{1,0:T(8,128)(2,1)} %refs_2_.3), custom_call_target="tpu_custom_call" | custom-call | flops 1000 | bytes 1000 | tf_op jit(solution)/shard_map/pallas_call | solution.py:38
  18.0 0.6 collective-permute-start.6
  18.7 1.2 %collective-permute-start.8 = (bf16[512,384]{1,0:T(8,128)(2,1)S(1)}, bf16[512,384]{1,0:T(8,128)(2,1)S(1)}, u32[]{:S(2)}, u32[]{:S(2)}) collective-permute-start(bf16[512,384]{1,0:T(8,128)(2,1)S(1)} %shard_map.147.refs_1_.refs_5_), channel_id=1, source_target_pairs={{0,4},{4,0},{8,12},{12,8},{1,5},{5,1},{9,13},{13,9},{2,6},{6,2},{1... | collective-permute-start | bytes 1179656 | tf_op jit(solution)/shard_map/ppermute | solution.py:26
  19.8 4.4 %collective-permute-done.3.refs_6_.refs_0_ = bf16[512,384]{1,0:T(8,128)(2,1)} collective-permute-done((bf16[512,384]{1,0:T(8,128)(2,1)}, bf16[512,384]{1,0:T(8,128)(2,1)}, u32[]{:S(2)}, u32[]{:S(2)}) %collective-permute-start.3) | collective-permute-done | bytes 393248 | tf_op jit(solution)/shard_map/ppermute | solution.py:26
  24.2 0.6 collective-permute-start.5
  24.8 0.6 collective-permute-start.11
  25.4 1.3 %shard_map.149.refs_9_.refs_5_.refs_2_ = bf16[384,1536]{1,0:T(8,128)(2,1)S(1)} custom-call(s32[1]{0:T(128)} %bitcast.me_ref, bf16[384,1536]{1,0:T(8,128)(2,1)} %source_ref.2), custom_call_target="tpu_custom_call" | custom-call | flops 1000 | bytes 1000 | tf_op jit(solution)/shard_map/pallas_call | solution.py:38
  26.7 2.5 %shard_map.148 = (bf16[1536,768]{1,0:T(8,128)(2,1)S(1)}, f32[2,768]{1,0:T(2,128)S(1)}) custom-call(s32[1]{0:T(128)} %bitcast.me_ref, f32[32,384]{1,0:T(8,128)S(1)} %all_gather.3.gains_ref, bf16[1536,384]{1,0:T(8,128)(2,1)} %refs_0_.7, bf16[1536,384]{1,0:T(8,128)(2,1)} %refs_1_.5), custom_call_target="tpu_custom_call" | custom-call | flops 1000 | bytes 1000 | tf_op jit(solution)/shard_map/pallas_call | solution.py:38
  29.3 3.0 %shard_map.150 = (bf16[512,768]{1,0:T(8,128)(2,1)S(1)}, bf16[512,384]{1,0:T(8,128)(2,1)S(1)}, bf16[512,768]{1,0:T(8,128)(2,1)S(1)}) custom-call(bf16[512,384]{1,0:T(8,128)(2,1)S(1)} %copy-done.6, bf16[512,384]{1,0:T(8,128)(2,1)S(1)} %shard_map.147.refs_1_.refs_5_, bf16[512,384]{1,0:T(8,128)(2,1)S(1)} %collective-permute-done.1.refs_2_.refs_6_, ...), custom_call_target="tpu_custom_call" | custom-call | flops 1000 | bytes 1000 | tf_op jit(solution)/shard_map/pallas_call | solution.py:38
  32.3 2.1 %collective-permute-done.6.refs_0_ = bf16[192,1536]{1,0:T(8,128)(2,1)S(1)} collective-permute-done((bf16[192,1536]{1,0:T(8,128)(2,1)}, bf16[192,1536]{1,0:T(8,128)(2,1)S(1)}, u32[]{:S(2)}, u32[]{:S(2)}) %collective-permute-start.6) | collective-permute-done | bytes 589856 | tf_op jit(solution)/shard_map/ppermute | solution.py:26
  34.4 2.2 %shard_map.153 = (f32[512,1536]{1,0:T(8,128)S(1)}, f32[8,128]{1,0:T(8,128)S(1)}) custom-call(bf16[512,768]{1,0:T(8,128)(2,1)S(1)} %get-tuple-element.36.query_ref, bf16[512,384]{1,0:T(8,128)(2,1)S(1)} %get-tuple-element.37.key_ref, bf16[512,768]{1,0:T(8,128)(2,1)S(1)} %get-tuple-element.38.value_ref, bf16[192,1536]{1,0:T(8,128)(2,1)S(1)} %collective-permute-done.6.refs_0_), custom_call_target="tpu_custom_call" | custom-call | flops 1000 | bytes 1000 | tf_op jit(solution)/shard_map/pallas_call | solution.py:38
  36.8 4.4 %collective-permute-done.5.refs_0_ = bf16[512,384]{1,0:T(8,128)(2,1)S(1)} collective-permute-done((bf16[512,384]{1,0:T(8,128)(2,1)}, bf16[512,384]{1,0:T(8,128)(2,1)S(1)}, u32[]{:S(2)}, u32[]{:S(2)}) %collective-permute-start.5) | collective-permute-done | bytes 393248 | tf_op jit(solution)/shard_map/ppermute | solution.py:26
  41.6 0.5 collective-permute-start.20
  42.3 1.5 %collective-permute-start.19 = (bf16[192,1536]{1,0:T(8,128)(2,1)S(1)}, bf16[192,1536]{1,0:T(8,128)(2,1)}, u32[]{:S(2)}, u32[]{:S(2)}) collective-permute-start(bf16[192,1536]{1,0:T(8,128)(2,1)S(1)} %shard_map.166.refs_9_), channel_id=1, source_target_pairs={{0,16},{16,0},{1,17},{17,1},{2,18},{18,2},{3,19},{19,3},{4,20},{20... | collective-permute-start | bytes 1769480 | tf_op jit(solution)/shard_map/ppermute | solution.py:26
  43.8 2.8 %shard_map.156 = (bf16[512,384]{1,0:T(8,128)(2,1)S(1)}, bf16[512,768]{1,0:T(8,128)(2,1)S(1)}) custom-call(bf16[512,384]{1,0:T(8,128)(2,1)} %collective-permute-done.4.refs_7_.refs_0_, bf16[512,384]{1,0:T(8,128)(2,1)S(1)} %shard_map.155.refs_1_, bf16[512,384]{1,0:T(8,128)(2,1)S(1)} %collective-permute-done.9.refs_2_, ...), custom_call_target="tpu_custom_call" | custom-call | flops 1000 | bytes 1000 | tf_op jit(solution)/shard_map/pallas_call | solution.py:38
  46.7 3.7 %shard_map.158 = (f32[512,1536]{1,0:T(8,128)S(1)}, f32[8,128]{1,0:T(8,128)S(1)}) custom-call(bf16[512,768]{1,0:T(8,128)(2,1)S(1)} %get-tuple-element.36.query_ref, bf16[512,384]{1,0:T(8,128)(2,1)S(1)} %get-tuple-element.40.key_ref, bf16[512,768]{1,0:T(8,128)(2,1)S(1)} %get-tuple-element.41.value_ref, ...), custom_call_target="tpu_custom_call", output_to_operand_aliasing={{0}: (3, {})} | custom-call | flops 1000 | bytes 1000 | tf_op jit(solution)/shard_map/pallas_call | solution.py:38
  50.4 1.8 %collective-permute-done.7.refs_0_ = bf16[512,384]{1,0:T(8,128)(2,1)S(1)} collective-permute-done((bf16[512,384]{1,0:T(8,128)(2,1)S(1)}, bf16[512,384]{1,0:T(8,128)(2,1)S(1)}, u32[]{:S(2)}, u32[]{:S(2)}) %collective-permute-start.7) | collective-permute-done | bytes 393248 | tf_op jit(solution)/shard_map/ppermute | solution.py:26
  52.2 0.5 collective-permute-start.13
  52.7 2.8 %shard_map.161 = (bf16[512,384]{1,0:T(8,128)(2,1)S(1)}, bf16[512,768]{1,0:T(8,128)(2,1)S(1)}) custom-call(bf16[512,384]{1,0:T(8,128)(2,1)} %collective-permute-done.3.refs_6_.refs_0_, bf16[512,384]{1,0:T(8,128)(2,1)S(1)} %shard_map.157.refs_2_.refs_1_, bf16[512,384]{1,0:T(8,128)(2,1)S(1)} %collective-permute-done.14.refs_2_, ...), custom_call_target="tpu_custom_call" | custom-call | flops 1000 | bytes 1000 | tf_op jit(solution)/shard_map/pallas_call | solution.py:38
  55.6 3.9 %shard_map.162 = (f32[512,1536]{1,0:T(8,128)S(1)}, f32[8,128]{1,0:T(8,128)}) custom-call(bf16[512,768]{1,0:T(8,128)(2,1)S(1)} %get-tuple-element.36.query_ref, bf16[512,384]{1,0:T(8,128)(2,1)S(1)} %get-tuple-element.46.key_ref, bf16[512,768]{1,0:T(8,128)(2,1)S(1)} %get-tuple-element.47.value_ref, ...), custom_call_target="tpu_custom_call", output_to_operand_aliasing={{0}: (3, {})} | custom-call | flops 1000 | bytes 1000 | tf_op jit(solution)/shard_map/pallas_call | solution.py:38
  59.5 1.9 %shard_map.160 = (bf16[512,384]{1,0:T(8,128)(2,1)S(1)}, bf16[512,768]{1,0:T(8,128)(2,1)S(1)}) custom-call(bf16[512,384]{1,0:T(8,128)(2,1)S(1)} %shard_map.154.refs_1_.refs_0_, bf16[512,384]{1,0:T(8,128)(2,1)S(1)} %shard_map.159.refs_1_, bf16[512,384]{1,0:T(8,128)(2,1)S(1)} %collective-permute-done.12.refs_2_, ...), custom_call_target="tpu_custom_call" | custom-call | flops 1000 | bytes 1000 | tf_op jit(solution)/shard_map/pallas_call | solution.py:38
  61.4 2.8 %shard_map.163.refs_1_.refs_0_ = bf16[256,384]{1,0:T(8,128)(2,1)} custom-call(bf16[512,768]{1,0:T(8,128)(2,1)S(1)} %get-tuple-element.36.query_ref, bf16[512,384]{1,0:T(8,128)(2,1)S(1)} %get-tuple-element.44.key_ref, bf16[512,768]{1,0:T(8,128)(2,1)S(1)} %get-tuple-element.45.value_ref, f32[512,1536]{1,0:T(8,128)S(1)} %get-tuple-element.49.refs_0_), custom_call_target="tpu_custom_call" | custom-call | flops 1000 | bytes 1000 | tf_op jit(solution)/shard_map/pallas_call | solution.py:38
  65.1 2.1 %shard_map.164.refs_1_.refs_0_ = bf16[256,384]{1,0:T(8,128)(2,1)S(1)} custom-call(bf16[512,768]{1,0:T(8,128)(2,1)S(1)} %get-tuple-element.36.query_ref, bf16[512,384]{1,0:T(8,128)(2,1)S(1)} %get-tuple-element.44.key_ref, bf16[512,768]{1,0:T(8,128)(2,1)S(1)} %get-tuple-element.45.value_ref, f32[512,1536]{1,0:T(8,128)S(1)} %get-tuple-element.49.refs_0_), custom_call_target="tpu_custom_call" | custom-call | flops 1000 | bytes 1000 | tf_op jit(solution)/shard_map/pallas_call | solution.py:38
  67.3 4.5 %collective-permute-done.16.refs_0_ = bf16[256,384]{1,0:T(8,128)(2,1)} collective-permute-done((bf16[256,384]{1,0:T(8,128)(2,1)}, bf16[256,384]{1,0:T(8,128)(2,1)}, u32[]{:S(2)}, u32[]{:S(2)}) %collective-permute-start.16) | collective-permute-done | bytes 196640 | tf_op jit(solution)/shard_map/ppermute | solution.py:26
  71.8 1.0 copy-done.3
  73.6 1.7 %copy-done.2 = bf16[1536,768]{1,0:T(8,128)(2,1)S(1)} copy-done((bf16[1536,768]{1,0:T(8,128)(2,1)S(1)}, bf16[1536,768]{1,0:T(8,128)(2,1)}, u32[]{:S(2)}) %copy-start.2) | copy-done | bytes 2359320
  75.3 1.3 %copy-done.4 = bf16[384,1536]{1,0:T(8,128)(2,1)S(1)} copy-done((bf16[384,1536]{1,0:T(8,128)(2,1)S(1)}, bf16[384,1536]{1,0:T(8,128)(2,1)}, u32[]{:S(2)}) %copy-start.4) | copy-done | bytes 1179672
  76.5 1.0 copy-done.7
  77.5 1.0 copy-done.9
  78.5 1.0 copy-done.11
  79.5 4.2 %shard_map.168 = (bf16[256,384]{1,0:T(8,128)(2,1)S(1)}, bf16[256,384]{1,0:T(8,128)(2,1)S(1)}, bf16[16,384]{1,0:T(8,128)(2,1)S(1)}, bf16[16,384]{1,0:T(8,128)(2,1)S(1)}) custom-call(s32[1]{0:T(128)} %bitcast.me_ref, s32[1]{0:T(128)} %bitcast.1.part_ref, s32[1]{0:T(128)} %bitcast.2.odd_ref.refs_0_, bf16[256,384]{1,0:T(8,128)(2,1)} %shard_map.163.refs_1_.refs_0_, ...), custom_call_target="tpu_custom_call" | custom-call | flops 1000 | bytes 1000 | tf_op jit(solution)/shard_map/pallas_call | solution.py:38
  84.1 1.3 %collective-permute-start.26 = (bf16[16,384]{1,0:T(8,128)(2,1)S(1)}, bf16[16,384]{1,0:T(8,128)(2,1)S(1)}, u32[]{:S(2)}, u32[]{:S(2)}) collective-permute-start(bf16[16,384]{1,0:T(8,128)(2,1)S(1)} %get-tuple-element.54), channel_id=1, source_target_pairs={{0,4},{4,0},{8,12},{12,8},{1,5},{5,1},{9,13},{13,9},{2,6},{6,2},{1... | collective-permute-start | bytes 36872 | tf_op jit(solution)/shard_map/ppermute | solution.py:26
  85.4 0.7 collective-permute-start.27
  86.1 4.6 %shard_map.170 = (bf16[256,384]{1,0:T(8,128)(2,1)S(1)}, bf16[256,384]{1,0:T(8,128)(2,1)S(1)}, bf16[16,384]{1,0:T(8,128)(2,1)}, bf16[16,384]{1,0:T(8,128)(2,1)}) custom-call(s32[1]{0:T(128)} %bitcast.me_ref, s32[1]{0:T(128)} %bitcast.1.part_ref, s32[1]{0:T(128)} %bitcast.2.odd_ref.refs_0_, bf16[256,384]{1,0:T(8,128)(2,1)S(1)} %shard_map.164.refs_1_.refs_0_, ...), custom_call_target="tpu_custom_call" | custom-call | flops 1000 | bytes 1000 | tf_op jit(solution)/shard_map/pallas_call | solution.py:38
  90.7 1.7 %shard_map.171 = (bf16[256,768]{1,0:T(8,128)(2,1)S(1)}, bf16[256,768]{1,0:T(8,128)(2,1)S(1)}) custom-call(bf16[256,384]{1,0:T(8,128)(2,1)S(1)} %get-tuple-element.52.refs_1_.first_ref, bf16[256,384]{1,0:T(8,128)(2,1)S(1)} %get-tuple-element.53.second_ref, s32[1]{0:T(128)} %bitcast.2.odd_ref.refs_0_, bf16[16,384]{1,0:T(8,128)(2,1)S(1)} %collective-permute-done.26.refs_1_, ...), custom_call_target="tpu_custom_call" | custom-call | flops 1000 | bytes 1000 | tf_op jit(solution)/shard_map/pallas_call | solution.py:38
  92.5 2.0 %shard_map.172 = (bf16[256,768]{1,0:T(8,128)(2,1)S(1)}, bf16[256,768]{1,0:T(8,128)(2,1)S(1)}) custom-call(bf16[256,384]{1,0:T(8,128)(2,1)S(1)} %get-tuple-element.52.refs_1_.first_ref, bf16[256,384]{1,0:T(8,128)(2,1)S(1)} %get-tuple-element.53.second_ref, f32[31,384]{1,0:T(8,128)S(1)} %copy-done.12, f32[2,384]{1,0:T(2,128)S(1)} %pad_maximum_fusion.1.refs_4_.refs_1_, ...), custom_call_target="tpu_custom_call" | custom-call | flops 1000 | bytes 1000 | tf_op jit(solution)/shard_map/pallas_call | solution.py:38
  94.5 0.6 collective-permute-start.30
  95.1 1.5 %collective-permute-start.29 = (bf16[256,384]{1,0:T(8,128)(2,1)S(1)}, bf16[256,384]{1,0:T(8,128)(2,1)S(1)}, u32[]{:S(2)}, u32[]{:S(2)}) collective-permute-start(bf16[256,384]{1,0:T(8,128)(2,1)S(1)} %add_convert_fusion.3), channel_id=1, source_target_pairs={{0,2},{1,3},{2,0},{3,1},{4,6},{5,7},{6,4},{7,5},{8,10},{9,11},{10,... | collective-permute-start | bytes 589832 | tf_op jit(solution)/shard_map/ppermute | solution.py:26
  96.7 1.3 %collective-permute-start.31 = (bf16[256,384]{1,0:T(8,128)(2,1)S(1)}, bf16[256,384]{1,0:T(8,128)(2,1)S(1)}, u32[]{:S(2)}, u32[]{:S(2)}) collective-permute-start(bf16[256,384]{1,0:T(8,128)(2,1)S(1)} %add_convert_fusion.1), channel_id=1, source_target_pairs={{0,2},{1,3},{2,0},{3,1},{4,6},{5,7},{6,4},{7,5},{8,10},{9,11},{10,... | collective-permute-start | bytes 589832 | tf_op jit(solution)/shard_map/ppermute | solution.py:26
  98.0 4.9 %collective-permute-done.29 = bf16[256,384]{1,0:T(8,128)(2,1)S(1)} collective-permute-done((bf16[256,384]{1,0:T(8,128)(2,1)S(1)}, bf16[256,384]{1,0:T(8,128)(2,1)S(1)}, u32[]{:S(2)}, u32[]{:S(2)}) %collective-permute-start.29) | collective-permute-done | bytes 196640 | tf_op jit(solution)/shard_map/ppermute | solution.py:26
  103.1 3.1 %collective-permute-done.31 = bf16[256,384]{1,0:T(8,128)(2,1)S(1)} collective-permute-done((bf16[256,384]{1,0:T(8,128)(2,1)S(1)}, bf16[256,384]{1,0:T(8,128)(2,1)S(1)}, u32[]{:S(2)}, u32[]{:S(2)}) %collective-permute-start.31) | collective-permute-done | bytes 196640 | tf_op jit(solution)/shard_map/ppermute | solution.py:26
  106.3 0.8 pad_maximum_fusion
  (84 shorter events, 3.4 us)
Async XLA Ops:
  0.0 18.0 %collective-permute-start = (bf16[512,384]{1,0:T(8,128)(2,1)}, bf16[512,384]{1,0:T(8,128)(2,1)S(1)}, u32[]{:S(2)}, u32[]{:S(2)}) collective-permute-start(bf16[512,384]{1,0:T(8,128)(2,1)} %refs_4_.3), channel_id=1, source_target_pairs={{0,2},{1,3},{2,0},{3,1},{4,6},{5,7},{6,4},{7,5},{8,10},{9,11},{10,... | collective-permute-start | bytes 1179656 | tf_op jit(solution)/shard_map/ppermute | solution.py:26
  2.9 15.7 %collective-permute-start.1 = (bf16[512,384]{1,0:T(8,128)(2,1)}, bf16[512,384]{1,0:T(8,128)(2,1)S(1)}, u32[]{:S(2)}, u32[]{:S(2)}) collective-permute-start(bf16[512,384]{1,0:T(8,128)(2,1)} %refs_4_.3), channel_id=1, source_target_pairs={{0,1},{1,0},{2,3},{3,2},{4,5},{5,4},{6,7},{7,6},{8,9},{9,8},{10,11... | collective-permute-start | bytes 1179656 | tf_op jit(solution)/shard_map/ppermute | solution.py:26
  2.9 21.3 %collective-permute-start.3 = (bf16[512,384]{1,0:T(8,128)(2,1)}, bf16[512,384]{1,0:T(8,128)(2,1)}, u32[]{:S(2)}, u32[]{:S(2)}) collective-permute-start(bf16[512,384]{1,0:T(8,128)(2,1)} %refs_4_.3), channel_id=1, source_target_pairs={{0,8},{4,12},{8,0},{12,4},{1,9},{5,13},{9,1},{13,5},{2,10},{6,14},... | collective-permute-start | bytes 1179656 | tf_op jit(solution)/shard_map/ppermute | solution.py:26
  5.5 19.3 %collective-permute-start.4 = (bf16[512,384]{1,0:T(8,128)(2,1)}, bf16[512,384]{1,0:T(8,128)(2,1)}, u32[]{:S(2)}, u32[]{:S(2)}) collective-permute-start(bf16[512,384]{1,0:T(8,128)(2,1)} %refs_4_.3), channel_id=1, source_target_pairs={{0,4},{4,0},{8,12},{12,8},{1,5},{5,1},{9,13},{13,9},{2,6},{6,2},{1... | collective-permute-start | bytes 1179656 | tf_op jit(solution)/shard_map/ppermute | solution.py:26
  18.0 16.4 %collective-permute-start.6 = (bf16[192,1536]{1,0:T(8,128)(2,1)}, bf16[192,1536]{1,0:T(8,128)(2,1)S(1)}, u32[]{:S(2)}, u32[]{:S(2)}) collective-permute-start(bf16[192,1536]{1,0:T(8,128)(2,1)} %shard_map.152), channel_id=1, source_target_pairs={{0,2},{1,3},{2,0},{3,1},{4,6},{5,7},{6,4},{7,5},{8,10},{9,11},{10,... | collective-permute-start | bytes 1769480 | tf_op jit(solution)/shard_map/ppermute | solution.py:26
  18.6 6.2 %collective-permute-start.2 = (bf16[512,384]{1,0:T(8,128)(2,1)S(1)}, bf16[512,384]{1,0:T(8,128)(2,1)S(1)}, u32[]{:S(2)}, u32[]{:S(2)}) collective-permute-start(bf16[512,384]{1,0:T(8,128)(2,1)S(1)} %shard_map.147.refs_1_.refs_5_), channel_id=1, source_target_pairs={{0,1},{1,0},{2,3},{3,2},{4,5},{5,4},{6,7},{7,6},{8,9},{9,8},{10,11... | collective-permute-start | bytes 1179656 | tf_op jit(solution)/shard_map/ppermute | solution.py:26
  18.7 10.6 %copy-start.8 = (bf16[512,384]{1,0:T(8,128)(2,1)}, bf16[512,384]{1,0:T(8,128)(2,1)S(1)}, u32[]{:S(2)}) copy-start(bf16[512,384]{1,0:T(8,128)(2,1)S(1)} %collective-permute-done.1.refs_2_.refs_6_) | copy-start | bytes 1179652
  18.7 18.0 %collective-permute-start.8 = (bf16[512,384]{1,0:T(8,128)(2,1)S(1)}, bf16[512,384]{1,0:T(8,128)(2,1)S(1)}, u32[]{:S(2)}, u32[]{:S(2)}) collective-permute-start(bf16[512,384]{1,0:T(8,128)(2,1)S(1)} %shard_map.147.refs_1_.refs_5_), channel_id=1, source_target_pairs={{0,4},{4,0},{8,12},{12,8},{1,5},{5,1},{9,13},{13,9},{2,6},{6,2},{1... | collective-permute-start | bytes 1179656 | tf_op jit(solution)/shard_map/ppermute | solution.py:26
  24.2 16.9 %collective-permute-start.5 = (bf16[512,384]{1,0:T(8,128)(2,1)}, bf16[512,384]{1,0:T(8,128)(2,1)S(1)}, u32[]{:S(2)}, u32[]{:S(2)}) collective-permute-start(bf16[512,384]{1,0:T(8,128)(2,1)} %collective-permute-done.3.refs_6_.refs_0_), channel_id=1, source_target_pairs={{0,4},{4,0},{8,12},{12,8},{1,5},{5,1},{9,13},{13,9},{2,6},{6,2},{1... | collective-permute-start | bytes 1179656 | tf_op jit(solution)/shard_map/ppermute | solution.py:26
  24.8 16.8 %collective-permute-start.9 = (bf16[512,384]{1,0:T(8,128)(2,1)}, bf16[512,384]{1,0:T(8,128)(2,1)S(1)}, u32[]{:S(2)}, u32[]{:S(2)}) collective-permute-start(bf16[512,384]{1,0:T(8,128)(2,1)} %collective-permute-done.4.refs_7_.refs_0_), channel_id=1, source_target_pairs={{0,1},{1,0},{2,3},{3,2},{4,5},{5,4},{6,7},{7,6},{8,9},{9,8},{10,11... | collective-permute-start | bytes 1179656 | tf_op jit(solution)/shard_map/ppermute | solution.py:26
  24.8 4.4 %copy-start.10 = (bf16[512,384]{1,0:T(8,128)(2,1)}, bf16[512,384]{1,0:T(8,128)(2,1)S(1)}, u32[]{:S(2)}) copy-start(bf16[512,384]{1,0:T(8,128)(2,1)S(1)} %collective-permute-done.2.refs_3_.refs_7_) | copy-start | bytes 1179652
  24.8 17.4 %collective-permute-start.11 = (bf16[512,384]{1,0:T(8,128)(2,1)}, bf16[512,384]{1,0:T(8,128)(2,1)S(1)}, u32[]{:S(2)}, u32[]{:S(2)}) collective-permute-start(bf16[512,384]{1,0:T(8,128)(2,1)} %collective-permute-done.3.refs_6_.refs_0_), channel_id=1, source_target_pairs={{0,2},{1,3},{2,0},{3,1},{4,6},{5,7},{6,4},{7,5},{8,10},{9,11},{10,... | collective-permute-start | bytes 1179656 | tf_op jit(solution)/shard_map/ppermute | solution.py:26
  26.7 2.5 %copy-start.6 = (bf16[512,384]{1,0:T(8,128)(2,1)S(1)}, bf16[512,384]{1,0:T(8,128)(2,1)}, u32[]{:S(2)}) copy-start(bf16[512,384]{1,0:T(8,128)(2,1)} %refs_4_.3) | copy-start | bytes 1179652
  29.2 3.1 %copy-start.1 = (bf16[1536,768]{1,0:T(8,128)(2,1)}, bf16[1536,768]{1,0:T(8,128)(2,1)S(1)}, u32[]{:S(2)}) copy-start(bf16[1536,768]{1,0:T(8,128)(2,1)S(1)} %get-tuple-element.50.refs_14_) | copy-start | bytes 7077892
  36.7 5.0 %copy-start = (bf16[384,1536]{1,0:T(8,128)(2,1)S(1)}, bf16[384,1536]{1,0:T(8,128)(2,1)}, u32[]{:S(2)}) copy-start(bf16[384,1536]{1,0:T(8,128)(2,1)} %refs_8_.3) | copy-start | bytes 3538948
  36.7 7.1 %collective-permute-start.10 = (bf16[512,384]{1,0:T(8,128)(2,1)S(1)}, bf16[512,384]{1,0:T(8,128)(2,1)S(1)}, u32[]{:S(2)}, u32[]{:S(2)}) collective-permute-start(bf16[512,384]{1,0:T(8,128)(2,1)S(1)} %shard_map.155.refs_1_), channel_id=1, source_target_pairs={{0,1},{1,0},{2,3},{3,2},{4,5},{5,4},{6,7},{7,6},{8,9},{9,8},{10,11... | collective-permute-start | bytes 1179656 | tf_op jit(solution)/shard_map/ppermute | solution.py:26
  41.2 11.0 %collective-permute-start.7 = (bf16[512,384]{1,0:T(8,128)(2,1)S(1)}, bf16[512,384]{1,0:T(8,128)(2,1)S(1)}, u32[]{:S(2)}, u32[]{:S(2)}) collective-permute-start(bf16[512,384]{1,0:T(8,128)(2,1)S(1)} %shard_map.154.refs_1_.refs_0_), channel_id=1, source_target_pairs={{0,2},{1,3},{2,0},{3,1},{4,6},{5,7},{6,4},{7,5},{8,10},{9,11},{10,... | collective-permute-start | bytes 1179656 | tf_op jit(solution)/shard_map/ppermute | solution.py:26
  41.6 10.5 %collective-permute-start.14 = (bf16[512,384]{1,0:T(8,128)(2,1)}, bf16[512,384]{1,0:T(8,128)(2,1)S(1)}, u32[]{:S(2)}, u32[]{:S(2)}) collective-permute-start(bf16[512,384]{1,0:T(8,128)(2,1)} %collective-permute-done.3.refs_6_.refs_0_), channel_id=1, source_target_pairs={{0,1},{1,0},{2,3},{3,2},{4,5},{5,4},{6,7},{7,6},{8,9},{9,8},{10,11... | collective-permute-start | bytes 1179656 | tf_op jit(solution)/shard_map/ppermute | solution.py:26
  41.6 30.2 %collective-permute-start.20 = (bf16[384,1536]{1,0:T(8,128)(2,1)S(1)}, bf16[384,1536]{1,0:T(8,128)(2,1)S(1)}, u32[]{:S(2)}, u32[]{:S(2)}) collective-permute-start(bf16[384,1536]{1,0:T(8,128)(2,1)S(1)} %copy-done), channel_id=1, source_target_pairs={{0,1},{1,0},{2,3},{3,2},{4,5},{5,4},{6,7},{7,6},{8,9},{9,8},{10,11... | collective-permute-start | bytes 3538952 | tf_op jit(solution)/shard_map/ppermute | solution.py:26
  42.3 21.9 %collective-permute-start.19 = (bf16[192,1536]{1,0:T(8,128)(2,1)S(1)}, bf16[192,1536]{1,0:T(8,128)(2,1)}, u32[]{:S(2)}, u32[]{:S(2)}) collective-permute-start(bf16[192,1536]{1,0:T(8,128)(2,1)S(1)} %shard_map.166.refs_9_), channel_id=1, source_target_pairs={{0,16},{16,0},{1,17},{17,1},{2,18},{18,2},{3,19},{19,3},{4,20},{20... | collective-permute-start | bytes 1769480 | tf_op jit(solution)/shard_map/ppermute | solution.py:26
  43.8 8.9 %collective-permute-start.15 = (bf16[512,384]{1,0:T(8,128)(2,1)S(1)}, bf16[512,384]{1,0:T(8,128)(2,1)S(1)}, u32[]{:S(2)}, u32[]{:S(2)}) collective-permute-start(bf16[512,384]{1,0:T(8,128)(2,1)S(1)} %shard_map.157.refs_2_.refs_1_), channel_id=1, source_target_pairs={{0,1},{1,0},{2,3},{3,2},{4,5},{5,4},{6,7},{7,6},{8,9},{9,8},{10,11... | collective-permute-start | bytes 1179656 | tf_op jit(solution)/shard_map/ppermute | solution.py:26
  52.2 7.3 %collective-permute-start.12 = (bf16[512,384]{1,0:T(8,128)(2,1)S(1)}, bf16[512,384]{1,0:T(8,128)(2,1)S(1)}, u32[]{:S(2)}, u32[]{:S(2)}) collective-permute-start(bf16[512,384]{1,0:T(8,128)(2,1)S(1)} %shard_map.154.refs_1_.refs_0_), channel_id=1, source_target_pairs={{0,1},{1,0},{2,3},{3,2},{4,5},{5,4},{6,7},{7,6},{8,9},{9,8},{10,11... | collective-permute-start | bytes 1179656 | tf_op jit(solution)/shard_map/ppermute | solution.py:26
  52.2 7.3 %collective-permute-start.13 = (bf16[512,384]{1,0:T(8,128)(2,1)S(1)}, bf16[512,384]{1,0:T(8,128)(2,1)S(1)}, u32[]{:S(2)}, u32[]{:S(2)}) collective-permute-start(bf16[512,384]{1,0:T(8,128)(2,1)S(1)} %shard_map.159.refs_1_), channel_id=1, source_target_pairs={{0,1},{1,0},{2,3},{3,2},{4,5},{5,4},{6,7},{7,6},{8,9},{9,8},{10,11... | collective-permute-start | bytes 1179656 | tf_op jit(solution)/shard_map/ppermute | solution.py:26
  52.7 20.7 %collective-permute-start.21 = (bf16[192,1536]{1,0:T(8,128)(2,1)S(1)}, bf16[192,1536]{1,0:T(8,128)(2,1)}, u32[]{:S(2)}, u32[]{:S(2)}) collective-permute-start(bf16[192,1536]{1,0:T(8,128)(2,1)S(1)} %shard_map.166.refs_9_), channel_id=1, source_target_pairs={{0,1},{1,0},{2,3},{3,2},{4,5},{5,4},{6,7},{7,6},{8,9},{9,8},{10,11... | collective-permute-start | bytes 1769480 | tf_op jit(solution)/shard_map/ppermute | solution.py:26
  64.2 9.4 %collective-permute-start.22 = (bf16[192,1536]{1,0:T(8,128)(2,1)}, bf16[192,1536]{1,0:T(8,128)(2,1)}, u32[]{:S(2)}, u32[]{:S(2)}) collective-permute-start(bf16[192,1536]{1,0:T(8,128)(2,1)} %shard_map.167.refs_10_), channel_id=1, source_target_pairs={{0,1},{1,0},{2,3},{3,2},{4,5},{5,4},{6,7},{7,6},{8,9},{9,8},{10,11... | collective-permute-start | bytes 1769480 | tf_op jit(solution)/shard_map/ppermute | solution.py:26
  64.6 7.2 %collective-permute-start.16 = (bf16[256,384]{1,0:T(8,128)(2,1)}, bf16[256,384]{1,0:T(8,128)(2,1)}, u32[]{:S(2)}, u32[]{:S(2)}) collective-permute-start(bf16[256,384]{1,0:T(8,128)(2,1)} %shard_map.163.refs_1_.refs_0_), channel_id=1, source_target_pairs={{0,2},{1,3},{2,0},{3,1},{4,6},{5,7},{6,4},{7,5},{8,10},{9,11},{10,... | collective-permute-start | bytes 589832 | tf_op jit(solution)/shard_map/ppermute | solution.py:26
  67.2 6.4 %collective-permute-start.17 = (bf16[256,384]{1,0:T(8,128)(2,1)}, bf16[256,384]{1,0:T(8,128)(2,1)}, u32[]{:S(2)}, u32[]{:S(2)}) collective-permute-start(bf16[256,384]{1,0:T(8,128)(2,1)} %shard_map.163.refs_1_.refs_0_), channel_id=1, source_target_pairs={{0,1},{1,0},{2,3},{3,2},{4,5},{5,4},{6,7},{7,6},{8,9},{9,8},{10,11... | collective-permute-start | bytes 589832 | tf_op jit(solution)/shard_map/ppermute | solution.py:26
  71.8 1.8 %collective-permute-start.18 = (bf16[256,384]{1,0:T(8,128)(2,1)}, bf16[256,384]{1,0:T(8,128)(2,1)}, u32[]{:S(2)}, u32[]{:S(2)}) collective-permute-start(bf16[256,384]{1,0:T(8,128)(2,1)} %shard_map.165.refs_1_), channel_id=1, source_target_pairs={{0,1},{1,0},{2,3},{3,2},{4,5},{5,4},{6,7},{7,6},{8,9},{9,8},{10,11... | collective-permute-start | bytes 589832 | tf_op jit(solution)/shard_map/ppermute | solution.py:26
  71.8 1.0 copy-start.3
  72.9 10.9 %collective-permute-start.23 = (bf16[256,384]{1,0:T(8,128)(2,1)S(1)}, bf16[256,384]{1,0:T(8,128)(2,1)}, u32[]{:S(2)}, u32[]{:S(2)}) collective-permute-start(bf16[256,384]{1,0:T(8,128)(2,1)S(1)} %shard_map.164.refs_1_.refs_0_), channel_id=1, source_target_pairs={{0,2},{1,3},{2,0},{3,1},{4,6},{5,7},{6,4},{7,5},{8,10},{9,11},{10,... | collective-permute-start | bytes 589832 | tf_op jit(solution)/shard_map/ppermute | solution.py:26
  73.3 12.8 %collective-permute-start.24 = (bf16[256,384]{1,0:T(8,128)(2,1)S(1)}, bf16[256,384]{1,0:T(8,128)(2,1)S(1)}, u32[]{:S(2)}, u32[]{:S(2)}) collective-permute-start(bf16[256,384]{1,0:T(8,128)(2,1)S(1)} %shard_map.164.refs_1_.refs_0_), channel_id=1, source_target_pairs={{0,1},{1,0},{2,3},{3,2},{4,5},{5,4},{6,7},{7,6},{8,9},{9,8},{10,11... | collective-permute-start | bytes 589832 | tf_op jit(solution)/shard_map/ppermute | solution.py:26
  73.6 1.7 %copy-start.2 = (bf16[1536,768]{1,0:T(8,128)(2,1)S(1)}, bf16[1536,768]{1,0:T(8,128)(2,1)}, u32[]{:S(2)}) copy-start(bf16[1536,768]{1,0:T(8,128)(2,1)} %copy-done.1) | copy-start | bytes 7077892
  75.3 1.3 %copy-start.4 = (bf16[384,1536]{1,0:T(8,128)(2,1)S(1)}, bf16[384,1536]{1,0:T(8,128)(2,1)}, u32[]{:S(2)}) copy-start(bf16[384,1536]{1,0:T(8,128)(2,1)} %copy-done.3) | copy-start | bytes 3538948
  76.5 1.0 copy-start.7
  77.5 1.0 copy-start.9
  78.5 1.0 copy-start.11
  79.5 4.6 %copy-start.13 = (f32[384]{0:T(512)S(1)}, f32[384]{0:T(512)}, u32[]{:S(2)}) copy-start(f32[384]{0:T(512)} %param.28) | copy-start | bytes 4612
  79.5 4.6 %copy-start.14 = (f32[384]{0:T(512)S(1)}, f32[384]{0:T(512)}, u32[]{:S(2)}) copy-start(f32[384]{0:T(512)} %param.27) | copy-start | bytes 4612
  79.5 6.6 %copy-start.5 = (bf16[384,1536]{1,0:T(8,128)(2,1)S(1)}, bf16[384,1536]{1,0:T(8,128)(2,1)}, u32[]{:S(2)}) copy-start(bf16[384,1536]{1,0:T(8,128)(2,1)} %copy-done.3) | copy-start | bytes 3538948
  83.8 2.3 %collective-permute-start.25 = (bf16[256,384]{1,0:T(8,128)(2,1)}, bf16[256,384]{1,0:T(8,128)(2,1)S(1)}, u32[]{:S(2)}, u32[]{:S(2)}) collective-permute-start(bf16[256,384]{1,0:T(8,128)(2,1)} %shard_map.169.refs_1_), channel_id=1, source_target_pairs={{0,1},{1,0},{2,3},{3,2},{4,5},{5,4},{6,7},{7,6},{8,9},{9,8},{10,11... | collective-permute-start | bytes 589832 | tf_op jit(solution)/shard_map/ppermute | solution.py:26
  84.1 6.6 %collective-permute-start.26 = (bf16[16,384]{1,0:T(8,128)(2,1)S(1)}, bf16[16,384]{1,0:T(8,128)(2,1)S(1)}, u32[]{:S(2)}, u32[]{:S(2)}) collective-permute-start(bf16[16,384]{1,0:T(8,128)(2,1)S(1)} %get-tuple-element.54), channel_id=1, source_target_pairs={{0,4},{4,0},{8,12},{12,8},{1,5},{5,1},{9,13},{13,9},{2,6},{6,2},{1... | collective-permute-start | bytes 36872 | tf_op jit(solution)/shard_map/ppermute | solution.py:26
  85.4 5.3 %collective-permute-start.27 = (bf16[16,384]{1,0:T(8,128)(2,1)S(1)}, bf16[16,384]{1,0:T(8,128)(2,1)S(1)}, u32[]{:S(2)}, u32[]{:S(2)}) collective-permute-start(bf16[16,384]{1,0:T(8,128)(2,1)S(1)} %get-tuple-element.55), channel_id=1, source_target_pairs={{4,8},{8,4},{5,9},{9,5},{6,10},{10,6},{7,11},{11,7},{20,24},{24,20... | collective-permute-start | bytes 36872 | tf_op jit(solution)/shard_map/ppermute | solution.py:537
  86.1 4.6 %copy-start.12 = (f32[31,384]{1,0:T(8,128)S(1)}, f32[31,384]{1,0:T(8,128)}, u32[]{:S(2)}) copy-start(f32[31,384]{1,0:T(8,128)} %refs_0_.9) | copy-start | bytes 142852
  92.4 2.6 %collective-permute-start.28 = (bf16[256,768]{1,0:T(8,128)(2,1)S(1)}, bf16[256,768]{1,0:T(8,128)(2,1)S(1)}, u32[]{:S(2)}, u32[]{:S(2)}) collective-permute-start(bf16[256,768]{1,0:T(8,128)(2,1)S(1)} %get-tuple-element.57), channel_id=1, source_target_pairs={{0,1},{1,0},{2,3},{3,2},{4,5},{5,4},{6,7},{7,6},{8,9},{9,8},{10,11... | collective-permute-start | bytes 1179656 | tf_op jit(solution)/shard_map/ppermute | solution.py:26
  94.5 2.2 %collective-permute-start.30 = (bf16[256,768]{1,0:T(8,128)(2,1)S(1)}, bf16[256,768]{1,0:T(8,128)(2,1)S(1)}, u32[]{:S(2)}, u32[]{:S(2)}) collective-permute-start(bf16[256,768]{1,0:T(8,128)(2,1)S(1)} %get-tuple-element.60), channel_id=1, source_target_pairs={{0,1},{1,0},{2,3},{3,2},{4,5},{5,4},{6,7},{7,6},{8,9},{9,8},{10,11... | collective-permute-start | bytes 1179656 | tf_op jit(solution)/shard_map/ppermute | solution.py:26
  95.1 7.8 %collective-permute-start.29 = (bf16[256,384]{1,0:T(8,128)(2,1)S(1)}, bf16[256,384]{1,0:T(8,128)(2,1)S(1)}, u32[]{:S(2)}, u32[]{:S(2)}) collective-permute-start(bf16[256,384]{1,0:T(8,128)(2,1)S(1)} %add_convert_fusion.3), channel_id=1, source_target_pairs={{0,2},{1,3},{2,0},{3,1},{4,6},{5,7},{6,4},{7,5},{8,10},{9,11},{10,... | collective-permute-start | bytes 589832 | tf_op jit(solution)/shard_map/ppermute | solution.py:26
  96.7 9.5 %collective-permute-start.31 = (bf16[256,384]{1,0:T(8,128)(2,1)S(1)}, bf16[256,384]{1,0:T(8,128)(2,1)S(1)}, u32[]{:S(2)}, u32[]{:S(2)}) collective-permute-start(bf16[256,384]{1,0:T(8,128)(2,1)S(1)} %add_convert_fusion.1), channel_id=1, source_target_pairs={{0,2},{1,3},{2,0},{3,1},{4,6},{5,7},{6,4},{7,5},{8,10},{9,11},{10,... | collective-permute-start | bytes 589832 | tf_op jit(solution)/shard_map/ppermute | solution.py:26
where the time goes:
time: 109 us; the launch traced here: 107 us
  Pallas kernels  47.1 us (43%)
  waiting for transfers between devices  25.5 us (23%)
  starting transfers between devices  20.7 us (19%)
  local copies, waits for them, and re-layouts  7.02 us (6%)
  blocking collectives  5.23 us (5%)
  other arithmetic  1.12 us (1%)
    pallas_call x18, Pallas kernels, kernel_call(): pl.pallas_call(body, in_specs=in_specs, out_specs=tuple((pl.BlockSpec(mem...  47.1 us
    ppermute x31, waiting for transfers between devices, exchange(): return lax.ppermute(cells, axis, [(i, i ^ distance) for i in range(count)])  25.5 us
    ppermute x31, starting transfers between devices, exchange(): return lax.ppermute(cells, axis, [(i, i ^ distance) for i in range(count)])  20.1 us
    unnamed x30, local copies, waits for them, and re-layouts  6.99 us
    all_gather x1, blocking collectives, on_device(): gains = lax.all_gather(gains, 'grid', axis=0, tiled=True)  5.23 us
  transfers between devices with their start and end apart: 32, of which 8 were waited for; matrix products, arithmetic and copies ran while one was open for 0% of the time, Pallas kernels for 42%

commit v1 on v0

--- a/solution.py
+++ b/solution.py
@@ -134,10 +134,10 @@
         copy.wait()
 
 
-def half_kernel(part_ref, source_ref, half_ref, done):
+def half_kernel(place_ref, source_ref, half_ref, done):
     rows = half_ref.shape[0]
     copy = pltpu.make_async_copy(
-        source_ref.at[pl.ds(pl.multiple_of(part_ref[0] * rows, rows), rows), :], half_ref, done.at[0]
+        source_ref.at[pl.ds(pl.multiple_of(place_ref[1] * rows, rows), rows), :], half_ref, done.at[0]
     )
     copy.start()
     copy.wait()
@@ -255,13 +255,13 @@
                 state_ref[:, at + PAIR : at + 2 * PAIR] = peak
 
 
-def middle_kernel(count, order, spans, me_ref, part_ref, odd_ref, *refs):
+def middle_kernel(count, order, spans, me_ref, *refs):
     attended, frames_refs, refs = refs[:count], refs[count : 2 * count], refs[2 * count :]
     *pieces, folded_ref, sums_ref, own_ref, out_ref, near_ref, far_ref, middle = refs
     total = out_ref.shape[0]
     width = frames_refs[0].shape[1]
     cells = jnp.concatenate([ref[:, :width] for ref in attended], axis=1)
-    swap = part_ref[0] != 0
+    swap = me_ref[1] != 0
 
     def weights(k):
         if width % PAIR:
@@ -294,7 +294,7 @@
         out_ref[:, j * PAIR : (j + 1) * PAIR] = (
             both[:, :PAIR] / (1.0 + jnp.exp(-both[:, PAIR:]))
         ).astype(BF16)
-    odd = odd_ref[0] != 0
+    odd = me_ref[2] != 0
     head, tail = out_ref[:HALO, :], out_ref[total - HALO :, :]
     near_ref[...] = jnp.where(odd, head, tail)
     far_ref[...] = jnp.where(odd, tail, head)
@@ -319,8 +319,8 @@
 
 def conv_kernel(outer, first_ref, second_ref, *refs):
     if outer:
-        odd_ref, near_ref, far_ref, *refs = refs
-        odd, near, far = odd_ref[0] != 0, near_ref[...], far_ref[...]
+        place_ref, near_ref, far_ref, *refs = refs
+        odd, near, far = place_ref[2] != 0, near_ref[...], far_ref[...]
     taps_ref, bn_ref, w_ref, keep_ref, send_ref, padded, activated = refs
     total, width = first_ref.shape
     half = keep_ref.shape[1]
@@ -382,8 +382,7 @@
     frames, width = frames_in.shape
     grid, ctx = lax.axis_size("grid"), lax.axis_size("ctx")
     me = lax.axis_index("grid")
-    place = me.astype(jnp.int32).reshape(1)
-    odd = (lax.axis_index("ctx") % 2).astype(jnp.int32).reshape(1)
+    place = jnp.stack([me, lax.axis_index("parts"), lax.axis_index("ctx") % 2]).astype(jnp.int32)
     order = list(range(0, grid, CORES)) + list(range(1, grid, CORES))
     padded = -(-width // PAIR) * PAIR
     every = ((0, frames),)
@@ -434,12 +433,11 @@
     glu, glu_sums = folded(place, order, 2, gains, (w_glu_value, w_glu_gate))
 
     parts = lax.axis_size("parts")
-    part = lax.axis_index("parts").astype(jnp.int32).reshape(1)
     if parts == 2:
         (half,) = kernel_call(
             half_kernel,
             [((width // 2, w_out.shape[1]), BF16)],
-            [part, w_out],
+            [place, w_out],
             spaces={0: pltpu.SMEM, 1: pltpu.HBM},
             scratch=[pltpu.SemaphoreType.DMA((1,))],
         )
@@ -525,8 +523,8 @@
         results = kernel_call(
             functools.partial(middle_kernel, n, order, spans[h]),
             [((rows, width), BF16), ((rows, padded), BF16), ((HALO, padded), BF16), ((HALO, padded), BF16)],
-            [place, part, odd, *mine, *other_core(mine), *own_blocks, *pieces, glu, glu_sums],
-            spaces={0: pltpu.SMEM, 1: pltpu.SMEM, 2: pltpu.SMEM},
+            [place, *mine, *other_core(mine), *own_blocks, *pieces, glu, glu_sums],
+            spaces={0: pltpu.SMEM},
             scratch=[pltpu.VMEM((rows, grid * width), BF16)],
         )
         middle.append(results[0])
@@ -536,7 +534,7 @@
             between = [(i, i + 1) for i in range(1, ctx - 1, 2)]
             far = lax.ppermute(results[3], "ctx", between + [(b, a) for a, b in between])
     outs = [None, None]
-    for h, around in ((1, []), (0, [odd, near, far])):
+    for h, around in ((1, []), (0, [place, near, far])):
         keep, send = kernel_call(
             functools.partial(conv_kernel, h == 0),
             [((rows, grid // CORES * width), BF16)] * 2,

time: 109 us -> 102 us (0.936)
  local copies, waits for them, and re-layouts: 7.02 us -> 0.05 us
  waiting for transfers between devices: 25.5 us -> 29.4 us
  Pallas kernels: 47.1 us -> 44.3 us
  starting transfers between devices: 20.7 us -> 19.5 us
    unnamed x30 -> x10, local copies, waits for them, and re-layouts: 6.99 us -> 0.03 us
    ppermute x31, waiting for transfers between devices: 25.5 us -> 29.4 us  [exchange(): return lax.ppermute(cells, axis, [(i, i ^ distance) for i in range(count)])]
    pallas_call x18, Pallas kernels: 47.1 us -> 44.3 us  [kernel_call(): pl.pallas_call(body, in_specs=in_specs, out_specs=tuple((pl.BlockSpec(mem...]
    ppermute x31, starting transfers between devices: 20.1 us -> 18.9 us  [exchange(): return lax.ppermute(cells, axis, [(i, i ^ distance) for i in range(count)])]
  transfers between devices with their start and end apart: 32 -> 32, of which waited for: 8 -> 11; matrix products, arithmetic and copies ran while one was open for 0% -> 0% of each run, Pallas kernels for 42% -> 42%
where the time goes in v1:
time: 102 us; the launch traced here: 100 us
  Pallas kernels  44.3 us (43%)
  waiting for transfers between devices  29.4 us (29%)
  starting transfers between devices  19.5 us (19%)
  blocking collectives  5.23 us (5%)
  other arithmetic  1.18 us (1%)
    pallas_call x18, Pallas kernels, kernel_call(): pl.pallas_call(body, in_specs=in_specs, out_specs=tuple((pl.BlockSpec(mem...  44.3 us
    ppermute x31, waiting for transfers between devices, exchange(): return lax.ppermute(cells, axis, [(i, i ^ distance) for i in range(count)])  29.4 us
    ppermute x31, starting transfers between devices, exchange(): return lax.ppermute(cells, axis, [(i, i ^ distance) for i in range(count)])  18.9 us
    all_gather x1, blocking collectives, on_device(): gains = lax.all_gather(gains, 'grid', axis=0, tiled=True)  5.23 us
  transfers between devices with their start and end apart: 32, of which 11 were waited for; matrix products, arithmetic and copies ran while one was open for 0% of the time, Pallas kernels for 42%

profile of v1, /device:TPU:0, one launch (start us, length us, event | category | flops | bytes accessed | tf_op | source)
XLA Modules:
  0.0 100.0 jit_solution(2315907767016121544)
XLA Ops:
  0.0 2.9 %collective-permute-start = (bf16[512,384]{1,0:T(8,128)(2,1)}, bf16[512,384]{1,0:T(8,128)(2,1)S(1)}, u32[]{:S(2)}, u32[]{:S(2)}) collective-permute-start(bf16[512,384]{1,0:T(8,128)(2,1)} %refs_4_.3), channel_id=1, source_target_pairs={{0,2},{1,3},{2,0},{3,1},{4,6},{5,7},{6,4},{7,5},{8,10},{9,11},{10,... | collective-permute-start | bytes 1179656 | tf_op jit(solution)/shard_map/ppermute | solution.py:26
  2.9 2.6 %collective-permute-start.3 = (bf16[512,384]{1,0:T(8,128)(2,1)}, bf16[512,384]{1,0:T(8,128)(2,1)S(1)}, u32[]{:S(2)}, u32[]{:S(2)}) collective-permute-start(bf16[512,384]{1,0:T(8,128)(2,1)} %refs_4_.3), channel_id=1, source_target_pairs={{0,8},{4,12},{8,0},{12,4},{1,9},{5,13},{9,1},{13,5},{2,10},{6,14},... | collective-permute-start | bytes 1179656 | tf_op jit(solution)/shard_map/ppermute | solution.py:26
  5.5 1.6 %collective-permute-start.4 = (bf16[512,384]{1,0:T(8,128)(2,1)}, bf16[512,384]{1,0:T(8,128)(2,1)S(1)}, u32[]{:S(2)}, u32[]{:S(2)}) collective-permute-start(bf16[512,384]{1,0:T(8,128)(2,1)} %refs_4_.3), channel_id=1, source_target_pairs={{0,4},{4,0},{8,12},{12,8},{1,5},{5,1},{9,13},{13,9},{2,6},{6,2},{1... | collective-permute-start | bytes 1179656 | tf_op jit(solution)/shard_map/ppermute | solution.py:26
  7.2 1.6 %shard_map.151.refs_0_ = bf16[192,1536]{1,0:T(8,128)(2,1)S(1)} custom-call(s32[3]{0:T(128)S(1)} %pad_add_fusion.me_ref.place_ref.refs_0_, bf16[384,1536]{1,0:T(8,128)(2,1)} %refs_8_.3), custom_call_target="tpu_custom_call" | custom-call | flops 1000 | bytes 1000 | tf_op jit(solution)/shard_map/pallas_call | solution.py:38
  8.8 0.8 shard_map.145
  9.6 5.2 %all_gather.3.gains_ref = f32[32,384]{1,0:T(8,128)S(1)} all-gather(f32[8,384]{1,0:T(8,128)S(1)} %shard_map.145), channel_id=1, replica_groups=mesh['parts'=2,'ctx'=4,'grid'=4] {'grid'}, dimensions={0}, use_global_device_ids=true | all-gather | bytes 61440 | tf_op jit(solution)/shard_map/all_gather | solution.py:409
  14.8 3.5 %shard_map.146 = (bf16[1536,1152]{1,0:T(8,128)(2,1)S(1)}, f32[2,1152]{1,0:T(2,128)S(1)}) custom-call(s32[3]{0:T(128)S(1)} %pad_add_fusion.me_ref.place_ref.refs_0_, f32[32,384]{1,0:T(8,128)S(1)} %all_gather.3.gains_ref, bf16[1536,384]{1,0:T(8,128)(2,1)} %refs_0_.6, bf16[1536,384]{1,0:T(8,128)(2,1)} %refs_1_.4, bf16[1536,384]{1,0:T(8,128)(2,1)} %refs_2_.3), custom_call_target="tpu_custom_call" | custom-call | flops 1000 | bytes 1000 | tf_op jit(solution)/shard_map/pallas_call | solution.py:38
  18.4 0.6 collective-permute-start.6
  19.0 1.3 %collective-permute-start.8 = (bf16[512,384]{1,0:T(8,128)(2,1)S(1)}, bf16[512,384]{1,0:T(8,128)(2,1)S(1)}, u32[]{:S(2)}, u32[]{:S(2)}) collective-permute-start(bf16[512,384]{1,0:T(8,128)(2,1)S(1)} %shard_map.147.refs_1_.refs_5_), channel_id=1, source_target_pairs={{0,4},{4,0},{8,12},{12,8},{1,5},{5,1},{9,13},{13,9},{2,6},{6,2},{1... | collective-permute-start | bytes 1179656 | tf_op jit(solution)/shard_map/ppermute | solution.py:26
  20.4 3.7 %collective-permute-done.3.refs_6_.refs_0_ = bf16[512,384]{1,0:T(8,128)(2,1)S(1)} collective-permute-done((bf16[512,384]{1,0:T(8,128)(2,1)}, bf16[512,384]{1,0:T(8,128)(2,1)S(1)}, u32[]{:S(2)}, u32[]{:S(2)}) %collective-permute-start.3) | collective-permute-done | bytes 393248 | tf_op jit(solution)/shard_map/ppermute | solution.py:26
  24.1 0.7 collective-permute-start.5
  24.8 0.6 collective-permute-start.11
  25.4 1.8 %shard_map.149.refs_9_.refs_5_.refs_2_ = bf16[384,1536]{1,0:T(8,128)(2,1)S(1)} custom-call(s32[3]{0:T(128)S(1)} %pad_add_fusion.me_ref.place_ref.refs_0_, bf16[384,1536]{1,0:T(8,128)(2,1)} %source_ref.2), custom_call_target="tpu_custom_call" | custom-call | flops 1000 | bytes 1000 | tf_op jit(solution)/shard_map/pallas_call | solution.py:38
  27.3 3.0 %shard_map.148 = (bf16[1536,768]{1,0:T(8,128)(2,1)S(1)}, f32[2,768]{1,0:T(2,128)S(1)}) custom-call(s32[3]{0:T(128)S(1)} %pad_add_fusion.me_ref.place_ref.refs_0_, f32[32,384]{1,0:T(8,128)S(1)} %all_gather.3.gains_ref, bf16[1536,384]{1,0:T(8,128)(2,1)} %refs_0_.7, bf16[1536,384]{1,0:T(8,128)(2,1)} %refs_1_.5), custom_call_target="tpu_custom_call" | custom-call | flops 1000 | bytes 1000 | tf_op jit(solution)/shard_map/pallas_call | solution.py:38
  30.3 3.0 %shard_map.150 = (bf16[512,768]{1,0:T(8,128)(2,1)S(1)}, bf16[512,384]{1,0:T(8,128)(2,1)S(1)}, bf16[512,768]{1,0:T(8,128)(2,1)S(1)}) custom-call(bf16[512,384]{1,0:T(8,128)(2,1)S(1)} %copy-done.1, bf16[512,384]{1,0:T(8,128)(2,1)S(1)} %shard_map.147.refs_1_.refs_5_, bf16[512,384]{1,0:T(8,128)(2,1)S(1)} %collective-permute-done.1.refs_2_.refs_6_, ...), custom_call_target="tpu_custom_call" | custom-call | flops 1000 | bytes 1000 | tf_op jit(solution)/shard_map/pallas_call | solution.py:38
  33.3 1.3 %collective-permute-done.6.refs_0_ = bf16[192,1536]{1,0:T(8,128)(2,1)S(1)} collective-permute-done((bf16[192,1536]{1,0:T(8,128)(2,1)S(1)}, bf16[192,1536]{1,0:T(8,128)(2,1)S(1)}, u32[]{:S(2)}, u32[]{:S(2)}) %collective-permute-start.6) | collective-permute-done | bytes 589856 | tf_op jit(solution)/shard_map/ppermute | solution.py:26
  34.6 2.2 %shard_map.153 = (f32[512,1536]{1,0:T(8,128)S(1)}, f32[8,128]{1,0:T(8,128)S(1)}) custom-call(bf16[512,768]{1,0:T(8,128)(2,1)S(1)} %get-tuple-element.36.query_ref, bf16[512,384]{1,0:T(8,128)(2,1)S(1)} %get-tuple-element.37.key_ref, bf16[512,768]{1,0:T(8,128)(2,1)S(1)} %get-tuple-element.38.value_ref, bf16[192,1536]{1,0:T(8,128)(2,1)S(1)} %collective-permute-done.6.refs_0_), custom_call_target="tpu_custom_call" | custom-call | flops 1000 | bytes 1000 | tf_op jit(solution)/shard_map/pallas_call | solution.py:38
  36.9 4.3 %collective-permute-done.5.refs_0_ = bf16[512,384]{1,0:T(8,128)(2,1)S(1)} collective-permute-done((bf16[512,384]{1,0:T(8,128)(2,1)S(1)}, bf16[512,384]{1,0:T(8,128)(2,1)S(1)}, u32[]{:S(2)}, u32[]{:S(2)}) %collective-permute-start.5) | collective-permute-done | bytes 393248 | tf_op jit(solution)/shard_map/ppermute | solution.py:26
  41.2 0.5 collective-permute-start.7
  41.6 0.5 collective-permute-start.20
  42.4 1.5 %collective-permute-start.19 = (bf16[192,1536]{1,0:T(8,128)(2,1)S(1)}, bf16[192,1536]{1,0:T(8,128)(2,1)S(1)}, u32[]{:S(2)}, u32[]{:S(2)}) collective-permute-start(bf16[192,1536]{1,0:T(8,128)(2,1)S(1)} %shard_map.166.refs_9_), channel_id=1, source_target_pairs={{0,16},{16,0},{1,17},{17,1},{2,18},{18,2},{3,19},{19,3},{4,20},{20... | collective-permute-start | bytes 1769480 | tf_op jit(solution)/shard_map/ppermute | solution.py:26
  44.0 1.9 %shard_map.156 = (bf16[512,384]{1,0:T(8,128)(2,1)S(1)}, bf16[512,768]{1,0:T(8,128)(2,1)S(1)}) custom-call(bf16[512,384]{1,0:T(8,128)(2,1)S(1)} %collective-permute-done.4.refs_7_.refs_0_, bf16[512,384]{1,0:T(8,128)(2,1)S(1)} %shard_map.155.refs_1_, bf16[512,384]{1,0:T(8,128)(2,1)S(1)} %collective-permute-done.9.refs_2_, ...), custom_call_target="tpu_custom_call" | custom-call | flops 1000 | bytes 1000 | tf_op jit(solution)/shard_map/pallas_call | solution.py:38
  45.8 3.7 %shard_map.158 = (f32[512,1536]{1,0:T(8,128)S(1)}, f32[8,128]{1,0:T(8,128)S(1)}) custom-call(bf16[512,768]{1,0:T(8,128)(2,1)S(1)} %get-tuple-element.36.query_ref, bf16[512,384]{1,0:T(8,128)(2,1)S(1)} %get-tuple-element.40.key_ref, bf16[512,768]{1,0:T(8,128)(2,1)S(1)} %get-tuple-element.41.value_ref, ...), custom_call_target="tpu_custom_call", output_to_operand_aliasing={{0}: (3, {})} | custom-call | flops 1000 | bytes 1000 | tf_op jit(solution)/shard_map/pallas_call | solution.py:38
  49.6 2.6 %collective-permute-done.7.refs_0_ = bf16[512,384]{1,0:T(8,128)(2,1)S(1)} collective-permute-done((bf16[512,384]{1,0:T(8,128)(2,1)S(1)}, bf16[512,384]{1,0:T(8,128)(2,1)S(1)}, u32[]{:S(2)}, u32[]{:S(2)}) %collective-permute-start.7) | collective-permute-done | bytes 393248 | tf_op jit(solution)/shard_map/ppermute | solution.py:26
  52.2 0.5 collective-permute-start.13
  52.7 1.8 %shard_map.161 = (bf16[512,384]{1,0:T(8,128)(2,1)S(1)}, bf16[512,768]{1,0:T(8,128)(2,1)S(1)}) custom-call(bf16[512,384]{1,0:T(8,128)(2,1)S(1)} %collective-permute-done.3.refs_6_.refs_0_, bf16[512,384]{1,0:T(8,128)(2,1)S(1)} %shard_map.157.refs_2_.refs_1_, bf16[512,384]{1,0:T(8,128)(2,1)S(1)} %collective-permute-done.14.refs_2_, ...), custom_call_target="tpu_custom_call" | custom-call | flops 1000 | bytes 1000 | tf_op jit(solution)/shard_map/pallas_call | solution.py:38
  54.6 3.9 %shard_map.162 = (f32[512,1536]{1,0:T(8,128)S(1)}, f32[8,128]{1,0:T(8,128)}) custom-call(bf16[512,768]{1,0:T(8,128)(2,1)S(1)} %get-tuple-element.36.query_ref, bf16[512,384]{1,0:T(8,128)(2,1)S(1)} %get-tuple-element.46.key_ref, bf16[512,768]{1,0:T(8,128)(2,1)S(1)} %get-tuple-element.47.value_ref, ...), custom_call_target="tpu_custom_call", output_to_operand_aliasing={{0}: (3, {})} | custom-call | flops 1000 | bytes 1000 | tf_op jit(solution)/shard_map/pallas_call | solution.py:38
  58.5 1.9 %shard_map.160 = (bf16[512,384]{1,0:T(8,128)(2,1)S(1)}, bf16[512,768]{1,0:T(8,128)(2,1)S(1)}) custom-call(bf16[512,384]{1,0:T(8,128)(2,1)S(1)} %shard_map.154.refs_1_.refs_0_, bf16[512,384]{1,0:T(8,128)(2,1)S(1)} %shard_map.159.refs_1_, bf16[512,384]{1,0:T(8,128)(2,1)S(1)} %collective-permute-done.12.refs_2_, ...), custom_call_target="tpu_custom_call" | custom-call | flops 1000 | bytes 1000 | tf_op jit(solution)/shard_map/pallas_call | solution.py:38
  60.4 2.1 %shard_map.163.refs_1_.refs_0_ = bf16[256,384]{1,0:T(8,128)(2,1)S(1)} custom-call(bf16[512,768]{1,0:T(8,128)(2,1)S(1)} %get-tuple-element.36.query_ref, bf16[512,384]{1,0:T(8,128)(2,1)S(1)} %get-tuple-element.44.key_ref, bf16[512,768]{1,0:T(8,128)(2,1)S(1)} %get-tuple-element.45.value_ref, f32[512,1536]{1,0:T(8,128)S(1)} %get-tuple-element.49.refs_0_), custom_call_target="tpu_custom_call" | custom-call | flops 1000 | bytes 1000 | tf_op jit(solution)/shard_map/pallas_call | solution.py:38
  62.5 0.5 collective-permute-start.22
  63.0 0.5 collective-permute-start.16
  63.5 2.1 %shard_map.164.refs_1_.refs_0_ = bf16[256,384]{1,0:T(8,128)(2,1)S(1)} custom-call(bf16[512,768]{1,0:T(8,128)(2,1)S(1)} %get-tuple-element.36.query_ref, bf16[512,384]{1,0:T(8,128)(2,1)S(1)} %get-tuple-element.44.key_ref, bf16[512,768]{1,0:T(8,128)(2,1)S(1)} %get-tuple-element.45.value_ref, f32[512,1536]{1,0:T(8,128)S(1)} %get-tuple-element.49.refs_0_), custom_call_target="tpu_custom_call" | custom-call | flops 1000 | bytes 1000 | tf_op jit(solution)/shard_map/pallas_call | solution.py:38
  65.9 4.0 %collective-permute-done.16.refs_0_ = bf16[256,384]{1,0:T(8,128)(2,1)S(1)} collective-permute-done((bf16[256,384]{1,0:T(8,128)(2,1)S(1)}, bf16[256,384]{1,0:T(8,128)(2,1)S(1)}, u32[]{:S(2)}, u32[]{:S(2)}) %collective-permute-start.16) | collective-permute-done | bytes 196640 | tf_op jit(solution)/shard_map/ppermute | solution.py:26
  69.9 0.5 collective-permute-start.23
  70.6 0.7 collective-permute-done.18.refs_3_
  71.3 3.1 %shard_map.168 = (bf16[256,384]{1,0:T(8,128)(2,1)S(1)}, bf16[256,384]{1,0:T(8,128)(2,1)S(1)}, bf16[16,384]{1,0:T(8,128)(2,1)S(1)}, bf16[16,384]{1,0:T(8,128)(2,1)S(1)}) custom-call(s32[3]{0:T(128)S(1)} %pad_add_fusion.me_ref.place_ref.refs_0_, bf16[256,384]{1,0:T(8,128)(2,1)S(1)} %shard_map.163.refs_1_.refs_0_, bf16[256,384]{1,0:T(8,128)(2,1)S(1)} %shard_map.165.refs_1_, ...), custom_call_target="tpu_custom_call" | custom-call | flops 1000 | bytes 1000 | tf_op jit(solution)/shard_map/pallas_call | solution.py:38
  74.4 2.8 %collective-permute-done.23.refs_0_ = bf16[256,384]{1,0:T(8,128)(2,1)S(1)} collective-permute-done((bf16[256,384]{1,0:T(8,128)(2,1)S(1)}, bf16[256,384]{1,0:T(8,128)(2,1)S(1)}, u32[]{:S(2)}, u32[]{:S(2)}) %collective-permute-start.23) | collective-permute-done | bytes 196640 | tf_op jit(solution)/shard_map/ppermute | solution.py:26
  77.2 1.2 %collective-permute-start.26 = (bf16[16,384]{1,0:T(8,128)(2,1)S(1)}, bf16[16,384]{1,0:T(8,128)(2,1)S(1)}, u32[]{:S(2)}, u32[]{:S(2)}) collective-permute-start(bf16[16,384]{1,0:T(8,128)(2,1)S(1)} %get-tuple-element.54), channel_id=1, source_target_pairs={{0,4},{4,0},{8,12},{12,8},{1,5},{5,1},{9,13},{13,9},{2,6},{6,2},{1... | collective-permute-start | bytes 36872 | tf_op jit(solution)/shard_map/ppermute | solution.py:26
  78.5 0.7 collective-permute-start.27
  79.2 3.7 %shard_map.170 = (bf16[256,384]{1,0:T(8,128)(2,1)S(1)}, bf16[256,384]{1,0:T(8,128)(2,1)S(1)}, bf16[16,384]{1,0:T(8,128)(2,1)}, bf16[16,384]{1,0:T(8,128)(2,1)}) custom-call(s32[3]{0:T(128)S(1)} %pad_add_fusion.me_ref.place_ref.refs_0_, bf16[256,384]{1,0:T(8,128)(2,1)S(1)} %shard_map.164.refs_1_.refs_0_, bf16[256,384]{1,0:T(8,128)(2,1)S(1)} %shard_map.169.refs_1_, ...), custom_call_target="tpu_custom_call" | custom-call | flops 1000 | bytes 1000 | tf_op jit(solution)/shard_map/pallas_call | solution.py:38
  82.9 2.2 %shard_map.171 = (bf16[256,768]{1,0:T(8,128)(2,1)S(1)}, bf16[256,768]{1,0:T(8,128)(2,1)S(1)}) custom-call(bf16[256,384]{1,0:T(8,128)(2,1)S(1)} %get-tuple-element.52.refs_1_.first_ref, bf16[256,384]{1,0:T(8,128)(2,1)S(1)} %get-tuple-element.53.second_ref, s32[3]{0:T(128)S(1)} %pad_add_fusion.me_ref.place_ref.refs_0_, ...), custom_call_target="tpu_custom_call" | custom-call | flops 1000 | bytes 1000 | tf_op jit(solution)/shard_map/pallas_call | solution.py:38
  85.4 2.0 %shard_map.172 = (bf16[256,768]{1,0:T(8,128)(2,1)S(1)}, bf16[256,768]{1,0:T(8,128)(2,1)S(1)}) custom-call(bf16[256,384]{1,0:T(8,128)(2,1)S(1)} %get-tuple-element.52.refs_1_.first_ref, bf16[256,384]{1,0:T(8,128)(2,1)S(1)} %get-tuple-element.53.second_ref, f32[31,384]{1,0:T(8,128)S(1)} %copy-done.2, f32[2,384]{1,0:T(2,128)S(1)} %pad_maximum_fusion.1.refs_4_.refs_1_, ...), custom_call_target="tpu_custom_call" | custom-call | flops 1000 | bytes 1000 | tf_op jit(solution)/shard_map/pallas_call | solution.py:38
  87.9 0.6 collective-permute-start.29
  88.4 0.8 collective-permute-done.30
  89.3 0.8 collective-permute-start.31
  90.1 5.6 %collective-permute-done.29 = bf16[256,384]{1,0:T(8,128)(2,1)S(1)} collective-permute-done((bf16[256,384]{1,0:T(8,128)(2,1)S(1)}, bf16[256,384]{1,0:T(8,128)(2,1)S(1)}, u32[]{:S(2)}, u32[]{:S(2)}) %collective-permute-start.29) | collective-permute-done | bytes 196640 | tf_op jit(solution)/shard_map/ppermute | solution.py:26
  95.8 3.3 %collective-permute-done.31 = bf16[256,384]{1,0:T(8,128)(2,1)S(1)} collective-permute-done((bf16[256,384]{1,0:T(8,128)(2,1)S(1)}, bf16[256,384]{1,0:T(8,128)(2,1)S(1)}, u32[]{:S(2)}, u32[]{:S(2)}) %collective-permute-start.31) | collective-permute-done | bytes 196640 | tf_op jit(solution)/shard_map/ppermute | solution.py:26
  99.3 0.8 pad_maximum_fusion
  (65 shorter events, 2.1 us)
Async XLA Ops:
  0.0 18.3 %collective-permute-start = (bf16[512,384]{1,0:T(8,128)(2,1)}, bf16[512,384]{1,0:T(8,128)(2,1)S(1)}, u32[]{:S(2)}, u32[]{:S(2)}) collective-permute-start(bf16[512,384]{1,0:T(8,128)(2,1)} %refs_4_.3), channel_id=1, source_target_pairs={{0,2},{1,3},{2,0},{3,1},{4,6},{5,7},{6,4},{7,5},{8,10},{9,11},{10,... | collective-permute-start | bytes 1179656 | tf_op jit(solution)/shard_map/ppermute | solution.py:26
  2.9 16.1 %collective-permute-start.1 = (bf16[512,384]{1,0:T(8,128)(2,1)}, bf16[512,384]{1,0:T(8,128)(2,1)S(1)}, u32[]{:S(2)}, u32[]{:S(2)}) collective-permute-start(bf16[512,384]{1,0:T(8,128)(2,1)} %refs_4_.3), channel_id=1, source_target_pairs={{0,1},{1,0},{2,3},{3,2},{4,5},{5,4},{6,7},{7,6},{8,9},{9,8},{10,11... | collective-permute-start | bytes 1179656 | tf_op jit(solution)/shard_map/ppermute | solution.py:26
  2.9 21.2 %collective-permute-start.3 = (bf16[512,384]{1,0:T(8,128)(2,1)}, bf16[512,384]{1,0:T(8,128)(2,1)S(1)}, u32[]{:S(2)}, u32[]{:S(2)}) collective-permute-start(bf16[512,384]{1,0:T(8,128)(2,1)} %refs_4_.3), channel_id=1, source_target_pairs={{0,8},{4,12},{8,0},{12,4},{1,9},{5,13},{9,1},{13,5},{2,10},{6,14},... | collective-permute-start | bytes 1179656 | tf_op jit(solution)/shard_map/ppermute | solution.py:26
  5.5 19.3 %collective-permute-start.4 = (bf16[512,384]{1,0:T(8,128)(2,1)}, bf16[512,384]{1,0:T(8,128)(2,1)S(1)}, u32[]{:S(2)}, u32[]{:S(2)}) collective-permute-start(bf16[512,384]{1,0:T(8,128)(2,1)} %refs_4_.3), channel_id=1, source_target_pairs={{0,4},{4,0},{8,12},{12,8},{1,5},{5,1},{9,13},{13,9},{2,6},{6,2},{1... | collective-permute-start | bytes 1179656 | tf_op jit(solution)/shard_map/ppermute | solution.py:26
  18.4 16.2 %collective-permute-start.6 = (bf16[192,1536]{1,0:T(8,128)(2,1)S(1)}, bf16[192,1536]{1,0:T(8,128)(2,1)S(1)}, u32[]{:S(2)}, u32[]{:S(2)}) collective-permute-start(bf16[192,1536]{1,0:T(8,128)(2,1)S(1)} %shard_map.152), channel_id=1, source_target_pairs={{0,2},{1,3},{2,0},{3,1},{4,6},{5,7},{6,4},{7,5},{8,10},{9,11},{10,... | collective-permute-start | bytes 1769480 | tf_op jit(solution)/shard_map/ppermute | solution.py:26
  19.0 5.9 %collective-permute-start.2 = (bf16[512,384]{1,0:T(8,128)(2,1)S(1)}, bf16[512,384]{1,0:T(8,128)(2,1)S(1)}, u32[]{:S(2)}, u32[]{:S(2)}) collective-permute-start(bf16[512,384]{1,0:T(8,128)(2,1)S(1)} %shard_map.147.refs_1_.refs_5_), channel_id=1, source_target_pairs={{0,1},{1,0},{2,3},{3,2},{4,5},{5,4},{6,7},{7,6},{8,9},{9,8},{10,11... | collective-permute-start | bytes 1179656 | tf_op jit(solution)/shard_map/ppermute | solution.py:26
  19.0 17.8 %collective-permute-start.8 = (bf16[512,384]{1,0:T(8,128)(2,1)S(1)}, bf16[512,384]{1,0:T(8,128)(2,1)S(1)}, u32[]{:S(2)}, u32[]{:S(2)}) collective-permute-start(bf16[512,384]{1,0:T(8,128)(2,1)S(1)} %shard_map.147.refs_1_.refs_5_), channel_id=1, source_target_pairs={{0,4},{4,0},{8,12},{12,8},{1,5},{5,1},{9,13},{13,9},{2,6},{6,2},{1... | collective-permute-start | bytes 1179656 | tf_op jit(solution)/shard_map/ppermute | solution.py:26
  24.1 17.0 %collective-permute-start.5 = (bf16[512,384]{1,0:T(8,128)(2,1)S(1)}, bf16[512,384]{1,0:T(8,128)(2,1)S(1)}, u32[]{:S(2)}, u32[]{:S(2)}) collective-permute-start(bf16[512,384]{1,0:T(8,128)(2,1)S(1)} %collective-permute-done.3.refs_6_.refs_0_), channel_id=1, source_target_pairs={{0,4},{4,0},{8,12},{12,8},{1,5},{5,1},{9,13},{13,9},{2,6},{6,2},{1... | collective-permute-start | bytes 1179656 | tf_op jit(solution)/shard_map/ppermute | solution.py:26
  24.8 16.8 %collective-permute-start.9 = (bf16[512,384]{1,0:T(8,128)(2,1)S(1)}, bf16[512,384]{1,0:T(8,128)(2,1)S(1)}, u32[]{:S(2)}, u32[]{:S(2)}) collective-permute-start(bf16[512,384]{1,0:T(8,128)(2,1)S(1)} %collective-permute-done.4.refs_7_.refs_0_), channel_id=1, source_target_pairs={{0,1},{1,0},{2,3},{3,2},{4,5},{5,4},{6,7},{7,6},{8,9},{9,8},{10,11... | collective-permute-start | bytes 1179656 | tf_op jit(solution)/shard_map/ppermute | solution.py:26
  24.8 17.6 %collective-permute-start.11 = (bf16[512,384]{1,0:T(8,128)(2,1)S(1)}, bf16[512,384]{1,0:T(8,128)(2,1)S(1)}, u32[]{:S(2)}, u32[]{:S(2)}) collective-permute-start(bf16[512,384]{1,0:T(8,128)(2,1)S(1)} %collective-permute-done.3.refs_6_.refs_0_), channel_id=1, source_target_pairs={{0,2},{1,3},{2,0},{3,1},{4,6},{5,7},{6,4},{7,5},{8,10},{9,11},{10,... | collective-permute-start | bytes 1179656 | tf_op jit(solution)/shard_map/ppermute | solution.py:26
  27.3 3.0 %copy-start.1 = (bf16[512,384]{1,0:T(8,128)(2,1)S(1)}, bf16[512,384]{1,0:T(8,128)(2,1)}, u32[]{:S(2)}) copy-start(bf16[512,384]{1,0:T(8,128)(2,1)} %refs_4_.3) | copy-start | bytes 1179652
  36.8 4.9 %copy-start = (bf16[384,1536]{1,0:T(8,128)(2,1)S(1)}, bf16[384,1536]{1,0:T(8,128)(2,1)}, u32[]{:S(2)}) copy-start(bf16[384,1536]{1,0:T(8,128)(2,1)} %refs_8_.3) | copy-start | bytes 3538948
  36.8 7.1 %collective-permute-start.10 = (bf16[512,384]{1,0:T(8,128)(2,1)S(1)}, bf16[512,384]{1,0:T(8,128)(2,1)S(1)}, u32[]{:S(2)}, u32[]{:S(2)}) collective-permute-start(bf16[512,384]{1,0:T(8,128)(2,1)S(1)} %shard_map.155.refs_1_), channel_id=1, source_target_pairs={{0,1},{1,0},{2,3},{3,2},{4,5},{5,4},{6,7},{7,6},{8,9},{9,8},{10,11... | collective-permute-start | bytes 1179656 | tf_op jit(solution)/shard_map/ppermute | solution.py:26
  41.2 11.0 %collective-permute-start.7 = (bf16[512,384]{1,0:T(8,128)(2,1)S(1)}, bf16[512,384]{1,0:T(8,128)(2,1)S(1)}, u32[]{:S(2)}, u32[]{:S(2)}) collective-permute-start(bf16[512,384]{1,0:T(8,128)(2,1)S(1)} %shard_map.154.refs_1_.refs_0_), channel_id=1, source_target_pairs={{0,2},{1,3},{2,0},{3,1},{4,6},{5,7},{6,4},{7,5},{8,10},{9,11},{10,... | collective-permute-start | bytes 1179656 | tf_op jit(solution)/shard_map/ppermute | solution.py:26
  41.6 10.5 %collective-permute-start.14 = (bf16[512,384]{1,0:T(8,128)(2,1)S(1)}, bf16[512,384]{1,0:T(8,128)(2,1)S(1)}, u32[]{:S(2)}, u32[]{:S(2)}) collective-permute-start(bf16[512,384]{1,0:T(8,128)(2,1)S(1)} %collective-permute-done.3.refs_6_.refs_0_), channel_id=1, source_target_pairs={{0,1},{1,0},{2,3},{3,2},{4,5},{5,4},{6,7},{7,6},{8,9},{9,8},{10,11... | collective-permute-start | bytes 1179656 | tf_op jit(solution)/shard_map/ppermute | solution.py:26
  41.6 28.2 %collective-permute-start.20 = (bf16[384,1536]{1,0:T(8,128)(2,1)S(1)}, bf16[384,1536]{1,0:T(8,128)(2,1)S(1)}, u32[]{:S(2)}, u32[]{:S(2)}) collective-permute-start(bf16[384,1536]{1,0:T(8,128)(2,1)S(1)} %copy-done), channel_id=1, source_target_pairs={{0,1},{1,0},{2,3},{3,2},{4,5},{5,4},{6,7},{7,6},{8,9},{9,8},{10,11... | collective-permute-start | bytes 3538952 | tf_op jit(solution)/shard_map/ppermute | solution.py:26
  42.4 20.0 %collective-permute-start.19 = (bf16[192,1536]{1,0:T(8,128)(2,1)S(1)}, bf16[192,1536]{1,0:T(8,128)(2,1)S(1)}, u32[]{:S(2)}, u32[]{:S(2)}) collective-permute-start(bf16[192,1536]{1,0:T(8,128)(2,1)S(1)} %shard_map.166.refs_9_), channel_id=1, source_target_pairs={{0,16},{16,0},{1,17},{17,1},{2,18},{18,2},{3,19},{19,3},{4,20},{20... | collective-permute-start | bytes 1769480 | tf_op jit(solution)/shard_map/ppermute | solution.py:26
  44.0 8.7 %collective-permute-start.15 = (bf16[512,384]{1,0:T(8,128)(2,1)S(1)}, bf16[512,384]{1,0:T(8,128)(2,1)S(1)}, u32[]{:S(2)}, u32[]{:S(2)}) collective-permute-start(bf16[512,384]{1,0:T(8,128)(2,1)S(1)} %shard_map.157.refs_2_.refs_1_), channel_id=1, source_target_pairs={{0,1},{1,0},{2,3},{3,2},{4,5},{5,4},{6,7},{7,6},{8,9},{9,8},{10,11... | collective-permute-start | bytes 1179656 | tf_op jit(solution)/shard_map/ppermute | solution.py:26
  52.2 6.3 %collective-permute-start.12 = (bf16[512,384]{1,0:T(8,128)(2,1)S(1)}, bf16[512,384]{1,0:T(8,128)(2,1)S(1)}, u32[]{:S(2)}, u32[]{:S(2)}) collective-permute-start(bf16[512,384]{1,0:T(8,128)(2,1)S(1)} %shard_map.154.refs_1_.refs_0_), channel_id=1, source_target_pairs={{0,1},{1,0},{2,3},{3,2},{4,5},{5,4},{6,7},{7,6},{8,9},{9,8},{10,11... | collective-permute-start | bytes 1179656 | tf_op jit(solution)/shard_map/ppermute | solution.py:26
  52.2 6.3 %collective-permute-start.13 = (bf16[512,384]{1,0:T(8,128)(2,1)S(1)}, bf16[512,384]{1,0:T(8,128)(2,1)S(1)}, u32[]{:S(2)}, u32[]{:S(2)}) collective-permute-start(bf16[512,384]{1,0:T(8,128)(2,1)S(1)} %shard_map.159.refs_1_), channel_id=1, source_target_pairs={{0,1},{1,0},{2,3},{3,2},{4,5},{5,4},{6,7},{7,6},{8,9},{9,8},{10,11... | collective-permute-start | bytes 1179656 | tf_op jit(solution)/shard_map/ppermute | solution.py:26
  52.7 17.8 %collective-permute-start.21 = (bf16[192,1536]{1,0:T(8,128)(2,1)S(1)}, bf16[192,1536]{1,0:T(8,128)(2,1)S(1)}, u32[]{:S(2)}, u32[]{:S(2)}) collective-permute-start(bf16[192,1536]{1,0:T(8,128)(2,1)S(1)} %shard_map.166.refs_9_), channel_id=1, source_target_pairs={{0,1},{1,0},{2,3},{3,2},{4,5},{5,4},{6,7},{7,6},{8,9},{9,8},{10,11... | collective-permute-start | bytes 1769480 | tf_op jit(solution)/shard_map/ppermute | solution.py:26
  62.5 8.8 %collective-permute-start.22 = (bf16[192,1536]{1,0:T(8,128)(2,1)S(1)}, bf16[192,1536]{1,0:T(8,128)(2,1)S(1)}, u32[]{:S(2)}, u32[]{:S(2)}) collective-permute-start(bf16[192,1536]{1,0:T(8,128)(2,1)S(1)} %shard_map.167.refs_10_), channel_id=1, source_target_pairs={{0,1},{1,0},{2,3},{3,2},{4,5},{5,4},{6,7},{7,6},{8,9},{9,8},{10,11... | collective-permute-start | bytes 1769480 | tf_op jit(solution)/shard_map/ppermute | solution.py:26
  63.0 6.9 %collective-permute-start.16 = (bf16[256,384]{1,0:T(8,128)(2,1)S(1)}, bf16[256,384]{1,0:T(8,128)(2,1)S(1)}, u32[]{:S(2)}, u32[]{:S(2)}) collective-permute-start(bf16[256,384]{1,0:T(8,128)(2,1)S(1)} %shard_map.163.refs_1_.refs_0_), channel_id=1, source_target_pairs={{0,2},{1,3},{2,0},{3,1},{4,6},{5,7},{6,4},{7,5},{8,10},{9,11},{10,... | collective-permute-start | bytes 589832 | tf_op jit(solution)/shard_map/ppermute | solution.py:26
  65.6 5.0 %collective-permute-start.17 = (bf16[256,384]{1,0:T(8,128)(2,1)S(1)}, bf16[256,384]{1,0:T(8,128)(2,1)S(1)}, u32[]{:S(2)}, u32[]{:S(2)}) collective-permute-start(bf16[256,384]{1,0:T(8,128)(2,1)S(1)} %shard_map.163.refs_1_.refs_0_), channel_id=1, source_target_pairs={{0,1},{1,0},{2,3},{3,2},{4,5},{5,4},{6,7},{7,6},{8,9},{9,8},{10,11... | collective-permute-start | bytes 589832 | tf_op jit(solution)/shard_map/ppermute | solution.py:26
  69.9 1.4 %collective-permute-start.18 = (bf16[256,384]{1,0:T(8,128)(2,1)S(1)}, bf16[256,384]{1,0:T(8,128)(2,1)S(1)}, u32[]{:S(2)}, u32[]{:S(2)}) collective-permute-start(bf16[256,384]{1,0:T(8,128)(2,1)S(1)} %shard_map.165.refs_1_), channel_id=1, source_target_pairs={{0,1},{1,0},{2,3},{3,2},{4,5},{5,4},{6,7},{7,6},{8,9},{9,8},{10,11... | collective-permute-start | bytes 589832 | tf_op jit(solution)/shard_map/ppermute | solution.py:26
  69.9 7.3 %collective-permute-start.23 = (bf16[256,384]{1,0:T(8,128)(2,1)S(1)}, bf16[256,384]{1,0:T(8,128)(2,1)S(1)}, u32[]{:S(2)}, u32[]{:S(2)}) collective-permute-start(bf16[256,384]{1,0:T(8,128)(2,1)S(1)} %shard_map.164.refs_1_.refs_0_), channel_id=1, source_target_pairs={{0,2},{1,3},{2,0},{3,1},{4,6},{5,7},{6,4},{7,5},{8,10},{9,11},{10,... | collective-permute-start | bytes 589832 | tf_op jit(solution)/shard_map/ppermute | solution.py:26
  70.4 8.7 %collective-permute-start.24 = (bf16[256,384]{1,0:T(8,128)(2,1)S(1)}, bf16[256,384]{1,0:T(8,128)(2,1)S(1)}, u32[]{:S(2)}, u32[]{:S(2)}) collective-permute-start(bf16[256,384]{1,0:T(8,128)(2,1)S(1)} %shard_map.164.refs_1_.refs_0_), channel_id=1, source_target_pairs={{0,1},{1,0},{2,3},{3,2},{4,5},{5,4},{6,7},{7,6},{8,9},{9,8},{10,11... | collective-permute-start | bytes 589832 | tf_op jit(solution)/shard_map/ppermute | solution.py:26
  71.3 5.9 %copy-start.3 = (f32[384]{0:T(512)S(1)}, f32[384]{0:T(512)}, u32[]{:S(2)}) copy-start(f32[384]{0:T(512)} %param.28) | copy-start | bytes 4612
  71.3 5.9 %copy-start.4 = (f32[384]{0:T(512)S(1)}, f32[384]{0:T(512)}, u32[]{:S(2)}) copy-start(f32[384]{0:T(512)} %param.27) | copy-start | bytes 4612
  77.2 2.0 %collective-permute-start.25 = (bf16[256,384]{1,0:T(8,128)(2,1)S(1)}, bf16[256,384]{1,0:T(8,128)(2,1)S(1)}, u32[]{:S(2)}, u32[]{:S(2)}) collective-permute-start(bf16[256,384]{1,0:T(8,128)(2,1)S(1)} %shard_map.169.refs_1_), channel_id=1, source_target_pairs={{0,1},{1,0},{2,3},{3,2},{4,5},{5,4},{6,7},{7,6},{8,9},{9,8},{10,11... | collective-permute-start | bytes 589832 | tf_op jit(solution)/shard_map/ppermute | solution.py:26
  77.2 5.7 %collective-permute-start.26 = (bf16[16,384]{1,0:T(8,128)(2,1)S(1)}, bf16[16,384]{1,0:T(8,128)(2,1)S(1)}, u32[]{:S(2)}, u32[]{:S(2)}) collective-permute-start(bf16[16,384]{1,0:T(8,128)(2,1)S(1)} %get-tuple-element.54), channel_id=1, source_target_pairs={{0,4},{4,0},{8,12},{12,8},{1,5},{5,1},{9,13},{13,9},{2,6},{6,2},{1... | collective-permute-start | bytes 36872 | tf_op jit(solution)/shard_map/ppermute | solution.py:26
  78.5 4.4 %collective-permute-start.27 = (bf16[16,384]{1,0:T(8,128)(2,1)S(1)}, bf16[16,384]{1,0:T(8,128)(2,1)S(1)}, u32[]{:S(2)}, u32[]{:S(2)}) collective-permute-start(bf16[16,384]{1,0:T(8,128)(2,1)S(1)} %get-tuple-element.55), channel_id=1, source_target_pairs={{4,8},{8,4},{5,9},{9,5},{6,10},{10,6},{7,11},{11,7},{20,24},{24,20... | collective-permute-start | bytes 36872 | tf_op jit(solution)/shard_map/ppermute | solution.py:535
  79.2 3.8 %copy-start.2 = (f32[31,384]{1,0:T(8,128)S(1)}, f32[31,384]{1,0:T(8,128)}, u32[]{:S(2)}) copy-start(f32[31,384]{1,0:T(8,128)} %refs_0_.9) | copy-start | bytes 142852
  85.2 2.7 %collective-permute-start.28 = (bf16[256,768]{1,0:T(8,128)(2,1)S(1)}, bf16[256,768]{1,0:T(8,128)(2,1)S(1)}, u32[]{:S(2)}, u32[]{:S(2)}) collective-permute-start(bf16[256,768]{1,0:T(8,128)(2,1)S(1)} %get-tuple-element.57), channel_id=1, source_target_pairs={{0,1},{1,0},{2,3},{3,2},{4,5},{5,4},{6,7},{7,6},{8,9},{9,8},{10,11... | collective-permute-start | bytes 1179656 | tf_op jit(solution)/shard_map/ppermute | solution.py:26
  87.4 1.8 %collective-permute-start.30 = (bf16[256,768]{1,0:T(8,128)(2,1)S(1)}, bf16[256,768]{1,0:T(8,128)(2,1)S(1)}, u32[]{:S(2)}, u32[]{:S(2)}) collective-permute-start(bf16[256,768]{1,0:T(8,128)(2,1)S(1)} %get-tuple-element.60), channel_id=1, source_target_pairs={{0,1},{1,0},{2,3},{3,2},{4,5},{5,4},{6,7},{7,6},{8,9},{9,8},{10,11... | collective-permute-start | bytes 1179656 | tf_op jit(solution)/shard_map/ppermute | solution.py:26
  87.9 7.8 %collective-permute-start.29 = (bf16[256,384]{1,0:T(8,128)(2,1)S(1)}, bf16[256,384]{1,0:T(8,128)(2,1)S(1)}, u32[]{:S(2)}, u32[]{:S(2)}) collective-permute-start(bf16[256,384]{1,0:T(8,128)(2,1)S(1)} %add_convert_fusion.3), channel_id=1, source_target_pairs={{0,2},{1,3},{2,0},{3,1},{4,6},{5,7},{6,4},{7,5},{8,10},{9,11},{10,... | collective-permute-start | bytes 589832 | tf_op jit(solution)/shard_map/ppermute | solution.py:26
  89.3 9.9 %collective-permute-start.31 = (bf16[256,384]{1,0:T(8,128)(2,1)S(1)}, bf16[256,384]{1,0:T(8,128)(2,1)S(1)}, u32[]{:S(2)}, u32[]{:S(2)}) collective-permute-start(bf16[256,384]{1,0:T(8,128)(2,1)S(1)} %add_convert_fusion.1), channel_id=1, source_target_pairs={{0,2},{1,3},{2,0},{3,1},{4,6},{5,7},{6,4},{7,5},{8,10},{9,11},{10,... | collective-permute-start | bytes 589832 | tf_op jit(solution)/shard_map/ppermute | solution.py:26
